TPU v7x, 256 devices: a whole 4x4x8 slice. The times are simulated.
256 devices in a mesh: row: 8 (over x, z_hi), col: 32 (over z_lo, y, core).
Axes of the slice: x: 4, y: 4, z: 8 (z_hi: 2, z_lo: 4; z = z_hi * 4 + z_lo), core: 2. Of those that a mesh axis runs over, the one named last changes fastest.
Arguments:
- activations: bfloat16 [3072, 8192], P(None, 'row'), may hold values from -6 to 6
- out_grads: bfloat16 [3072, 8192], P(None, 'col'), may hold values from -6 to 6
- act_basis: bfloat16 [8192, 8192], P('row', 'col'), may hold values from -0.0625 to 0.0625
- grad_basis: bfloat16 [8192, 8192], P('col', 'row'), may hold values from -0.0625 to 0.0625
Outputs:
- eigen_diag: float32 [8192, 8192], P('row', 'col')
All inputs are finite; a program needn't handle non-finite values.
Results may differ from a plain program's by a relative error of at most 0.0029.
Values may be sent and summed in bfloat16 or wider, within the bound.
No kernel may reach another device: no remote copies, remote signals or barrier semaphores. Data moves between devices by JAX's collectives and lax.ppermute only.
A program may use at most 64 MiB of HBM per device.

v0:
```python
import jax
import jax.numpy as jnp
from jax import lax
from jax.sharding import PartitionSpec as P

LEN = 512


def shards(activations, out_grads, act_basis, grad_basis):
    seq_count = activations.shape[0] // LEN
    scale = 1.0 / jnp.sqrt(jnp.float32(LEN))
    act_part = jnp.dot(activations, act_basis, preferred_element_type=jnp.float32)
    act_rot = lax.psum(act_part, "row").astype(jnp.bfloat16)
    grad_share = lax.psum_scatter(
        jnp.dot(out_grads, grad_basis, preferred_element_type=jnp.float32),
        "col",
        scatter_dimension=0,
        tiled=True,
    ).astype(jnp.bfloat16)
    grad_rot = lax.all_gather(grad_share, "col", axis=0, tiled=True)
    act_rot, grad_rot = (act_rot, grad_rot)
    grad_seq = grad_rot.reshape(-1, LEN, grad_rot.shape[1])
    act_seq = act_rot.reshape(-1, LEN, act_rot.shape[1])
    rotated = (
        jnp.einsum("slr,slc->rc", grad_seq[:1], act_seq[:1], preferred_element_type=jnp.float32)
        * scale
    )
    total = rotated * rotated
    for index in range(1, grad_seq.shape[0]):
        rotated = (
            jnp.einsum(
                "lr,lc->rc", grad_seq[index], act_seq[index], preferred_element_type=jnp.float32
            )
            * scale
        )
        total = total + rotated * rotated
    return total / jnp.float32(seq_count)


def solution(mesh):
    return jax.shard_map(
        shards,
        mesh=mesh,
        in_specs=(P(None, "row"), P(None, "col"), P("row", "col"), P("col", "row")),
        out_specs=P("row", "col"),
        check_vma=False,
    )
```

profile of v0, /device:TPU:1, one launch (start us, length us, event | category | flops | bytes accessed | tf_op | source)
XLA Modules:
  0.0 481.1 jit_solution(8421603355745097605)
XLA Ops:
  6.5 0.0 copy-start
  6.5 0.0 reduce-scatter.2.cloned.1.call-start
  6.5 1.4 copy-done
  7.9 7.4 %fusion.24 = f32[3072,1024]{1,0:T(8,128)} fusion(bf16[3072,256]{1,0:T(8,128)(2,1)S(1)} %copy-done, bf16[256,1024]{1,0:T(8,128)(2,1)} %param.7), kind=kOutput, calls=%fused_computation.30 | convolution fusion | flops 1610612736 | bytes 14680064 | tf_op jit(solution)/shard_map/dot_general | solution.py:15
  15.3 0.0 copy-start.2
  15.3 0.0 reduce-scatter.2.cloned.1.call-update
  15.4 0.0 all-gather.2.cloned.1.call-start
  15.4 175.0 %reduce-scatter.2.cloned.1.call-done = f32[96,1024]{1,0:T(8,128)} async-done(((f32[3072,1024]{1,0:T(8,128)}), f32[96,1024]{1,0:T(8,128)}) %reduce-scatter.2.cloned.1.call-update) | async-done | bytes 393232 | tf_op jit(solution)/shard_map/reduce_scatter | solution.py:14
  190.4 1.7 convert_element_type.6
  192.1 0.0 all-gather.2.cloned.1.call-update
  192.1 0.0 copy-done.2
  192.1 6.3 %fusion.25 = f32[3072,256]{1,0:T(8,128)} fusion(bf16[3072,1024]{1,0:T(8,128)(2,1)} %param.4, bf16[1024,256]{1,0:T(8,128)(2,1)S(1)} %copy-done.2), kind=kOutput, calls=%fused_computation.31 | convolution fusion | flops 1610612736 | bytes 9961472 | tf_op jit(solution)/shard_map/dot_general | solution.py:12
  198.4 230.9 %all-reduce.1 = bf16[3072,256]{1,0:T(8,128)(2,1)S(1)} all-reduce(f32[3072,256]{1,0:T(8,128)} %fusion.25), channel_id=1, replica_groups=mesh['row'=8,'col'=32] {'row'}, use_global_device_ids=true, to_apply=%region_1.0 | all-reduce | flops 786432 | bytes 4718592 | tf_op jit(solution)/shard_map/psum | solution.py:13
  429.3 38.2 %all-gather.2.cloned.1.call-done = bf16[3072,1024]{1,0:T(8,128)(2,1)} async-done(((bf16[96,1024]{1,0:T(8,128)(2,1)}), bf16[3072,1024]{1,0:T(8,128)(2,1)}) %all-gather.2.cloned.1.call-update) | async-done | bytes 6291472 | tf_op jit(solution)/shard_map/all_gather | solution.py:20
  467.6 0.0 copy-start.1
  467.6 1.8 fusion.11
  469.4 2.0 fusion.10
  471.4 0.0 copy-done.1
  471.4 0.5 fusion.8
  471.9 0.5 fusion.6
  472.4 0.5 fusion.4
  472.8 1.4 fusion.2
Async XLA Ops:
  6.5 1.4 copy-start
  6.5 183.8 %reduce-scatter.2.cloned.1.call-start = ((), (), s32[]{:S(2)}) async-start(), calls=%async_computation.1 | async-start | bytes 12976128 | tf_op jit(solution)/shard_map/reduce_scatter | solution.py:14
  15.3 176.8 %copy-start.2 = (bf16[1024,256]{1,0:T(8,128)(2,1)S(1)}, bf16[1024,256]{1,0:T(8,128)(2,1)}, u32[]{:S(2)}) copy-start(bf16[1024,256]{1,0:T(8,128)(2,1)} %param.6) | copy-start | bytes 1572868
  15.4 452.2 %all-gather.2.cloned.1.call-start = ((), (), s32[]{:S(2)}) async-start(), calls=%async_computation.2 | async-start | bytes 6488064 | tf_op jit(solution)/shard_map/all_gather | solution.py:20
  467.6 3.8 copy-start.1
Sparse Core Ops, SparseCore 0:
  15.5 174.8 reduce-scatter.1
  192.2 275.2 all-gather.1
where the time goes:
time: 483 us; the launch traced here: 481 us
  blocking collectives  231 us (48%)
  waiting for transfers between devices  213 us (44%)
  matrix products  20.4 us (4%)
  between operations  13.5 us (3%)
    psum x1, blocking collectives, shards(): act_rot = lax.psum(act_part, 'row').astype(jnp.bfloat16)  231 us
    reduce_scatter x1, waiting for transfers between devices, shards(): lax.psum_scatter(jnp.dot(out_grads, grad_basis, preferred_element_type=jn...  175 us
    all_gather x1, waiting for transfers between devices, shards(): grad_rot = lax.all_gather(grad_share, 'col', axis=0, tiled=True)  38.2 us
  transfers between devices with their start and end apart: 2, of which 2 were waited for; matrix products, arithmetic and copies ran while one was open for 1% of the time, Pallas kernels for 0%

commit v1 on v0

v1 whole, which is shorter than its diff:
```python
import functools

import jax
import jax.numpy as jnp
from jax import lax
from jax.experimental import pallas as pl
from jax.experimental.pallas import tpu as pltpu
from jax.sharding import PartitionSpec as P

LEN = 512
SEQS, HALF, QUARTER, PIECE, STEP = 3, 1536, 384, 96, 32
TAIL = 16
PAIRS = 2
F32, BF16 = jnp.float32, jnp.bfloat16


def col_swap(a, y=0, z=0, core=0):
    perm = [(i, i ^ (z * 8 + y * 2 + core)) for i in range(32)]
    return lax.ppermute(a, "col", perm)


def row_swap(a, x=0, z=0):
    perm = [(i, i ^ (x * 2 + z)) for i in range(8)]
    return lax.ppermute(a, "row", perm)


def exponent(v):
    return jnp.maximum(jnp.floor(jnp.log2(jnp.max(jnp.abs(v), keepdims=True))) + 2.0, -100.0)


def put(ref, v):
    rows = v.shape[0]
    e = exponent(v)
    t = v * jnp.exp2(16.0 - e)
    t = t * t
    t = t * t
    t = t * t
    ref[0:rows, :] = jnp.where(v < 0, -t, t).astype(BF16)
    ref[rows : rows + TAIL, :] = jnp.broadcast_to(e, (TAIL, ref.shape[1])).astype(BF16)


def get(ref, rows=None):
    end = ref.shape[0]
    e = ref[end - TAIL : end, :][0:1, 0:1].astype(F32)
    c = ref[slice(0, end - TAIL) if rows is None else rows, :].astype(F32)
    t = jnp.exp2(jnp.log2(jnp.abs(c)) * 0.125 + (e - 16.0))
    return jnp.where(c < 0, -t, t)


def quarter_rows(ref, q):
    rows = []
    for z in range(4):
        for s in range(SEQS):
            at = pl.multiple_of(s * LEN + q * (4 * STEP) + z * STEP, STEP)
            rows.append(ref[pl.ds(at, STEP), :])
    return jnp.concatenate(rows, 0)


def call(body, place, outs, ins, specs=None, name=None, flops=0, scratch=()):
    specs = specs or {}

    def whole(shape):
        return pl.BlockSpec(shape, lambda i, s: (0,) * len(shape))

    nbytes = sum(a.size * a.dtype.itemsize for a in ins) + sum(
        functools.reduce(lambda a, b: a * b, s, 1) * jnp.dtype(d).itemsize for s, d in outs
    )
    return pl.pallas_call(
        body,
        out_shape=[jax.ShapeDtypeStruct(s, d) for s, d in outs],
        grid_spec=pltpu.PrefetchScalarGridSpec(
            num_scalar_prefetch=1,
            grid=(1,),
            in_specs=[specs.get(i) or whole(a.shape) for i, a in enumerate(ins)],
            out_specs=[whole(s) for s, _ in outs],
            scratch_shapes=scratch,
        ),
        compiler_params=pltpu.CompilerParams(vmem_limit_bytes=24 * 2**20),
        cost_estimate=pl.CostEstimate(flops=flops, bytes_accessed=nbytes, transcendentals=0),
        name=name,
    )(place, *ins)


def grad_dot(own, got, gb_own, gb_got, q):
    p = jnp.dot(quarter_rows(own, q), gb_own[...], preferred_element_type=F32)
    return p + jnp.dot(quarter_rows(got, q), gb_got[...], preferred_element_type=F32)


def grad_first(place, own, got, gb_own, gb_got, send_a, send_b):
    p = grad_dot(own, got, gb_own, gb_got, place[2] ^ 2)
    w = p.shape[1] // (2 * PAIRS)
    for kind, ref in enumerate((send_a, send_b)):
        put(ref, jnp.concatenate([p[:, (2 * i + kind) * w : (2 * i + kind + 1) * w] for i in range(PAIRS)], 1))


def grad_rest(place, own, got, gb_own, gb_got, p1, p3, p0):
    for j, ref in ((1, p1), (3, p3), (0, p0)):
        ref[...] = grad_dot(own, got, gb_own, gb_got, place[2] ^ j)


def grad_second(place, p1, p3, got_a, got_b, send_p, send_q):
    w = got_a.shape[1]
    put(send_p, jnp.concatenate([p1[:, :w] + get(got_a), p1[:, w:]], 1))
    put(send_q, jnp.concatenate([p3[:, :w], p3[:, w:] + get(got_b)], 1))


def grad_z(place, p0, got_p, got_q, send1, send2, send3, keep):
    for k, ref in ((1, send1), (2, send2), (3, send3), (0, keep)):
        rows = pl.ds(pl.multiple_of((place[3] ^ k) * PIECE, STEP), PIECE)
        v = p0[rows, :] + get(got_p, rows) + get(got_q, rows)
        if k:
            put(ref, v)
        else:
            ref[...] = v


def grad_round(place, own, got1, got2, got3, out):
    out[...] = (own[...] + get(got1) + get(got2) + get(got3)).astype(BF16)


def grad_join(place, g0, g1, g2, g3, out):
    w = out.shape[2]
    for k, ref in enumerate((g0, g1, g2, g3)):
        for kind in range(2):
            out[kind, k * PIECE : (k + 1) * PIECE, :] = ref[:, kind * w : (kind + 1) * w]


def act_first(place, acts, ab_own, ab_got, send1, send2, send3, keep):
    for k, ref in ((1, send1), (2, send2), (3, send3), (0, keep)):
        rows = quarter_rows(acts, place[1] ^ k)
        v = jnp.concatenate([jnp.dot(rows, ab[...], preferred_element_type=F32) for ab in (ab_own, ab_got)], 1)
        if k:
            put(ref, v)
        else:
            ref[...] = v


def act_second(place, keep, got1, got2, got3, send, total):
    v = keep[...]
    for ref in (got1, got2, got3):
        v = v + get(ref)
    total[...] = v
    put(send, v)


def act_round(place, total, got, out):
    out[...] = (total[...] + get(got)).astype(BF16)


def act_join(place, a0, a1, a2, a3, out):
    for i, ref in enumerate((a0, a1, a2, a3)):
        j = place[1] ^ place[2] ^ i
        for z in range(4):
            for s in range(SEQS):
                at = pl.multiple_of((j * 4 + (place[3] ^ z)) * STEP, STEP)
                out[s, pl.ds(at, STEP), :] = ref[z * PIECE + s * STEP : z * PIECE + (s + 1) * STEP, :]


def square(place, acts, g, g_p, g_q, far_a, far_b, own, away):
    w, cols = g.shape[2], own.shape[1]
    for kind, far in enumerate((far_a, far_b)):
        total = None
        for s in range(SEQS):
            rows = []
            for ref in (g.at[kind], g_p.at[kind], far, g_q.at[kind]):
                for k in range(4):
                    at = k * PIECE + s * STEP
                    rows.append(ref[at : at + STEP, :])
            r = lax.dot_general(
                jnp.concatenate(rows, 0), acts[s], (((0,), (0,)), ((), ())), preferred_element_type=F32
            ) * F32(LEN**-0.5)
            total = r * r if total is None else total + r * r
        own[kind * w : (kind + 1) * w, :] = total[:, :cols]
        away[kind * w : (kind + 1) * w, :] = total[:, cols:]


def mean(place, *refs):
    out, parts = refs[-1], refs[:-1]
    rows = parts[0].shape[0]
    for i in range(len(parts) // 2):
        out[i * rows : (i + 1) * rows, :] = (parts[2 * i][...] + parts[2 * i + 1][...]) / F32(2 * SEQS)


def after(a, *others):
    return lax.optimization_barrier((a, *others))[0]


def shards(activations, out_grads, act_basis, grad_basis):
    row, col = lax.axis_index("row"), lax.axis_index("col")
    core = col % 2
    place = jnp.stack([core, row // 2, (col // 2) % 4, col // 8]).astype(jnp.int32)
    feats, dirs = grad_basis.shape
    cols = act_basis.shape[1]
    w = dirs // (2 * PAIRS)

    def columns(shape, index):
        return pl.BlockSpec(shape, lambda i, s: (0, index))

    def core_half(n):
        return pl.BlockSpec((HALF, n), lambda i, s: (s[0], 0))

    ab_got = col_swap(act_basis, core=1)
    og_got = col_swap(after(out_grads, ab_got), core=1)
    gb_got = col_swap(after(grad_basis, ab_got), core=1)

    a_shape = (QUARTER, 2 * cols)
    a_send = ((QUARTER + TAIL, 2 * cols), BF16)
    acts_feats = activations.shape[1]
    *a_sends, a_keep = call(
        act_first,
        place,
        [a_send] * 3 + [(a_shape, F32)],
        (activations, act_basis, ab_got),
        {0: core_half(acts_feats)},
        "act_first",
        2 * HALF * acts_feats * 2 * cols,
    )
    a_got = [row_swap(a, x=k) for k, a in zip((1, 2, 3), a_sends)]

    grad_ins = (out_grads, og_got, grad_basis, gb_got)
    grad_specs = {0: core_half(feats), 1: core_half(feats)}
    grad_flops = 2 * QUARTER * 2 * feats * dirs
    send_a, send_b = call(
        grad_first,
        after(place, a_keep),
        [((QUARTER + TAIL, dirs // 2), BF16)] * 2,
        grad_ins,
        grad_specs,
        "grad_first",
        grad_flops,
    )
    got_a, got_b = col_swap(send_a, y=3), col_swap(send_b, y=1)

    p1, p3, p0 = call(
        grad_rest,
        after(place, send_a),
        [((QUARTER, dirs), F32)] * 3,
        grad_ins,
        grad_specs,
        "grad_rest",
        3 * grad_flops,
    )

    got_p, got_q = [], []
    token = p0
    for pair in range(PAIRS):
        wide, narrow = columns((QUARTER, 2 * w), pair), columns((QUARTER + TAIL, w), pair)
        send_p, send_q = call(
            grad_second,
            after(place, token),
            [((QUARTER + TAIL, 2 * w), BF16)] * 2,
            (p1, p3, got_a, got_b),
            {0: wide, 1: wide, 2: narrow, 3: narrow},
            f"grad_second{pair}",
        )
        token = send_p
        got_p.append(col_swap(send_p, y=1))
        got_q.append(col_swap(send_q, y=3))

    a_send2, a_total = call(
        act_second, after(place, token), [a_send, (a_shape, F32)], (a_keep, *a_got), None, "act_second"
    )
    a_got2 = row_swap(a_send2, z=1)
    token = a_total

    keeps, z_gots = [], []
    for pair in range(PAIRS):
        *z_sends, keep = call(
            grad_z,
            after(place, token),
            [((PIECE + TAIL, 2 * w), BF16)] * 3 + [((PIECE, 2 * w), F32)],
            (p0, got_p[pair], got_q[pair]),
            {0: columns((QUARTER, 2 * w), pair)},
            f"grad_z{pair}",
        )
        token = keep
        keeps.append(keep)
        z_gots.append([col_swap(a, z=k) for k, a in zip((1, 2, 3), z_sends)])

    g_all = []
    for pair in range(PAIRS):
        (g_own,) = call(
            grad_round,
            after(place, token),
            [((PIECE, 2 * w), BF16)],
            (keeps[pair], *z_gots[pair]),
            None,
            f"grad_round{pair}",
        )
        token = g_own
        g_all.append([g_own, *[col_swap(g_own, z=k) for k in (1, 2, 3)]])
        if pair == 0:
            (a_own,) = call(
                act_round, after(place, token), [(a_shape, BF16)], (a_total, a_got2), None, "act_round"
            )
            token = a_own
            a_all = [a_own, *[row_swap(a_own, x=k) for k in (1, 2, 3)]]

    gs = []
    for pair in range(PAIRS):
        (g,) = call(
            grad_join, after(place, token), [((2, QUARTER, w), BF16)], g_all[pair], None, f"grad_join{pair}"
        )
        token = g
        gs.append((g, col_swap(g, y=1), col_swap(g, y=3)))
        if pair == 0:
            (acts,) = call(
                act_join, after(place, token), [((SEQS, LEN, 2 * cols), BF16)], a_all, None, "act_join"
            )
            token = acts

    parts = []
    for pair in range(PAIRS):
        g, g_p, g_q = gs[pair]
        far_a, far_b = col_swap(g_p[0], y=3), col_swap(g_q[1], y=1)
        own, away = call(
            square,
            place,
            [((2 * w, cols), F32)] * 2,
            (acts, g, g_p, g_q, far_a, far_b),
            None,
            f"square{pair}",
            2 * HALF * 2 * w * 2 * cols,
        )
        parts += [own, col_swap(away, core=1)]
    (out,) = call(mean, place, [((dirs, cols), F32)], parts, None, "mean")
    return out


def solution(mesh):
    return jax.shard_map(
        shards,
        mesh=mesh,
        in_specs=(P(None, "row"), P(None, "col"), P("row", "col"), P("col", "row")),
        out_specs=P("row", "col"),
        check_vma=False,
    )
```

time: 483 us -> 139 us (0.29)
  blocking collectives: 231 us -> 0 us
  waiting for transfers between devices: 213 us -> 52.5 us
  starting transfers between devices: 0.04 us -> 56.7 us
  Pallas kernels: 0 us -> 25.7 us
  matrix products: 20.4 us -> 0 us
  between operations: 13.5 us -> 0.24 us
    psum x1 -> x0, blocking collectives: 231 us -> none  [shards(): act_rot = lax.psum(act_part, 'row').astype(jnp.bfloat16)]
    reduce_scatter x1 -> x0, waiting for transfers between devices: 175 us -> none  [shards(): lax.psum_scatter(jnp.dot(out_grads, grad_basis, preferred_element_type=jn...]
    ppermute x0 -> x38, starting transfers between devices: none -> 56.7 us  [the longest x31 45.1 us: col_swap(): return lax.ppermute(a, 'col', perm)]
    ppermute x0 -> x38, waiting for transfers between devices: none -> 52.5 us  [the longest x31 46.9 us: col_swap(): return lax.ppermute(a, 'col', perm)]
    all_gather x1 -> x0, waiting for transfers between devices: 38.2 us -> none  [shards(): grad_rot = lax.all_gather(grad_share, 'col', axis=0, tiled=True)]
    pallas_call x0 -> x17, Pallas kernels: none -> 25.7 us  [call(): pl.pallas_call(body, out_shape=[jax.ShapeDtypeStruct(s, d) for s, d in ou...]
    dot_general x8 -> x0, matrix products: 20.4 us -> none  [the longest x1 7.39 us: shards(): jnp.dot(out_grads, grad_basis, preferred_element_type=jnp.float32)]
  transfers between devices with their start and end apart: 2 -> 38, of which waited for: 2 -> 14; matrix products, arithmetic and copies ran while one was open for 1% -> 0% of each run, Pallas kernels for 0% -> 16%
where the time goes in v1:
time: 139 us
  starting transfers between devices  56.7 us (41%)
  waiting for transfers between devices  52.5 us (38%)
  Pallas kernels  25.7 us (18%)
  local copies, waits for them, and re-layouts  3.89 us (3%)
    ppermute x31, waiting for transfers between devices, col_swap(): return lax.ppermute(a, 'col', perm)  46.9 us
    ppermute x31, starting transfers between devices, col_swap(): return lax.ppermute(a, 'col', perm)  45.1 us
    pallas_call x17, Pallas kernels, call(): pl.pallas_call(body, out_shape=[jax.ShapeDtypeStruct(s, d) for s, d in ou...  25.7 us
    ppermute x7, starting transfers between devices, row_swap(): return lax.ppermute(a, 'row', perm)  11.6 us
    ppermute x7, waiting for transfers between devices, row_swap(): return lax.ppermute(a, 'row', perm)  5.56 us
    unnamed x8, local copies, waits for them, and re-layouts  3.83 us
  transfers between devices with their start and end apart: 38, of which 14 were waited for; matrix products, arithmetic and copies ran while one was open for 0% of the time, Pallas kernels for 16%

profile of v1, /device:TPU:1, one launch (start us, length us, event | category | flops | bytes accessed | tf_op | source)
XLA Modules:
  0.0 139.2 jit_solution(16565738667158517844)
XLA Ops:
  0.0 3.2 %collective-permute-start = (bf16[1024,256]{1,0:T(8,128)(2,1)}, bf16[1024,256]{1,0:T(8,128)(2,1)S(1)}, u32[]{:S(2)}, u32[]{:S(2)}) collective-permute-start(bf16[1024,256]{1,0:T(8,128)(2,1)} %ab_own.1), channel_id=1, source_target_pairs={{0,1},{1,0},{2,3},{3,2},{4,5},{5,4},{6,7},{7,6},{8,9},{9,8},{10,11... | collective-permute-start | bytes 1572872 | tf_op jit(solution)/shard_map/ppermute | solution.py:19
  3.2 1.7 %collective-permute-done.ab_got = bf16[1024,256]{1,0:T(8,128)(2,1)S(1)} collective-permute-done((bf16[1024,256]{1,0:T(8,128)(2,1)}, bf16[1024,256]{1,0:T(8,128)(2,1)S(1)}, u32[]{:S(2)}, u32[]{:S(2)}) %collective-permute-start) | collective-permute-done | bytes 524320 | tf_op jit(solution)/shard_map/ppermute | solution.py:19
  5.0 0.4 collective-permute-start.1
  5.4 0.1 collective-permute-start.2
  5.6 2.8 %copy-done = bf16[3072,1024]{1,0:T(8,128)(2,1)S(1)} copy-done((bf16[3072,1024]{1,0:T(8,128)(2,1)S(1)}, bf16[3072,1024]{1,0:T(8,128)(2,1)}, u32[]{:S(2)}) %copy-start) | copy-done | bytes 6291480
  8.4 1.0 copy-done.3
  9.4 3.4 %act_first.1 = (bf16[400,512]{1,0:T(8,128)(2,1)S(1)}, bf16[400,512]{1,0:T(8,128)(2,1)S(1)}, bf16[400,512]{1,0:T(8,128)(2,1)S(1)}, f32[384,512]{1,0:T(8,128)S(1)}) custom-call(s32[4]{0:T(128)S(1)} %pad_add_fusion.place, bf16[3072,1024]{1,0:T(8,128)(2,1)S(1)} %copy-done, bf16[1024,256]{1,0:T(8,128)(2,1)S(1)} %copy-done.3, ...), custom_call_target="tpu_custom_call" | custom-call | flops 1610612736 | bytes 9355264 | tf_op jit(solution)/shard_map/act_first/pallas_call | solution.py:68
  12.9 1.9 %grad_first.1 = (bf16[400,512]{1,0:T(8,128)(2,1)S(1)}, bf16[400,512]{1,0:T(8,128)(2,1)S(1)}) custom-call(s32[4]{0:T(128)S(1)} %pad_add_fusion.place, bf16[3072,256]{1,0:T(8,128)(2,1)S(1)} %copy-done.1, bf16[3072,256]{1,0:T(8,128)(2,1)S(1)} %collective-permute-done.1.got, bf16[256,1024]{1,0:T(8,128)(2,1)S(1)} %copy-done.2, ...), custom_call_target="tpu_custom_call" | custom-call | flops 402653184 | bytes 5013504 | tf_op jit(solution)/shard_map/grad_first/pallas_call | solution.py:68
  14.8 1.4 %collective-permute-start.3 = (bf16[400,512]{1,0:T(8,128)(2,1)S(1)}, bf16[400,512]{1,0:T(8,128)(2,1)S(1)}, u32[]{:S(2)}, u32[]{:S(2)}) collective-permute-start(bf16[400,512]{1,0:T(8,128)(2,1)S(1)} %get-tuple-element.51), channel_id=1, source_target_pairs={{0,6},{1,7},{2,4},{3,5},{4,2},{5,3},{6,0},{7,1},{8,14},{9,15},{10,... | collective-permute-start | bytes 1228808 | tf_op jit(solution)/shard_map/ppermute | solution.py:19
  16.3 1.2 collective-permute-start.5
  17.5 2.4 %collective-permute-start.6 = (bf16[400,512]{1,0:T(8,128)(2,1)S(1)}, bf16[400,512]{1,0:T(8,128)(2,1)S(1)}, u32[]{:S(2)}, u32[]{:S(2)}) collective-permute-start(bf16[400,512]{1,0:T(8,128)(2,1)S(1)} %get-tuple-element.63), channel_id=1, source_target_pairs={{0,128},{32,160},{64,192},{96,224},{128,0},{160,32},{192,64},{224,... | collective-permute-start | bytes 1228808 | tf_op jit(solution)/shard_map/ppermute | solution.py:24
  19.9 0.2 collective-permute-start.7
  20.1 1.9 %grad_rest.1 = (f32[384,1024]{1,0:T(8,128)S(1)}, f32[384,1024]{1,0:T(8,128)S(1)}, f32[384,1024]{1,0:T(8,128)S(1)}) custom-call(s32[4]{0:T(128)S(1)} %pad_add_fusion.place, bf16[3072,256]{1,0:T(8,128)(2,1)S(1)} %copy-done.1, bf16[3072,256]{1,0:T(8,128)(2,1)S(1)} %collective-permute-done.1.got, bf16[256,1024]{1,0:T(8,128)(2,1)S(1)} %copy-done.2, ...), custom_call_target="tpu_custom_call" | custom-call | flops 1207959552 | bytes 8912896 | tf_op jit(solution)/shard_map/grad_rest/pallas_call | solution.py:68
  22.1 3.4 %collective-permute-done.4.got_b = bf16[400,512]{1,0:T(8,128)(2,1)S(1)} collective-permute-done((bf16[400,512]{1,0:T(8,128)(2,1)S(1)}, bf16[400,512]{1,0:T(8,128)(2,1)S(1)}, u32[]{:S(2)}, u32[]{:S(2)}) %collective-permute-start.4) | collective-permute-done | bytes 409632 | tf_op jit(solution)/shard_map/ppermute | solution.py:19
  25.5 1.3 collective-permute-done.3.got_a
  26.8 1.8 %grad_second0.1 = (bf16[400,512]{1,0:T(8,128)(2,1)S(1)}, bf16[400,512]{1,0:T(8,128)(2,1)S(1)}) custom-call(s32[4]{0:T(128)S(1)} %pad_add_fusion.place, f32[384,1024]{1,0:T(8,128)S(1)} %get-tuple-element.55.p1, f32[384,1024]{1,0:T(8,128)S(1)} %get-tuple-element.56.p3, bf16[400,512]{1,0:T(8,128)(2,1)S(1)} %collective-permute-done.3.got_a, ...), custom_call_target="tpu_custom_call" | custom-call | bytes 4784128 | tf_op jit(solution)/shard_map/grad_second0/pallas_call | solution.py:68
  28.6 1.1 collective-permute-start.9
  29.7 1.8 %grad_second1.1 = (bf16[400,512]{1,0:T(8,128)(2,1)S(1)}, bf16[400,512]{1,0:T(8,128)(2,1)S(1)}) custom-call(s32[4]{0:T(128)S(1)} %pad_add_fusion.place, f32[384,1024]{1,0:T(8,128)S(1)} %get-tuple-element.55.p1, f32[384,1024]{1,0:T(8,128)S(1)} %get-tuple-element.56.p3, bf16[400,512]{1,0:T(8,128)(2,1)S(1)} %collective-permute-done.3.got_a, ...), custom_call_target="tpu_custom_call" | custom-call | bytes 4784128 | tf_op jit(solution)/shard_map/grad_second1/pallas_call | solution.py:68
  31.5 1.9 %collective-permute-start.11 = (bf16[400,512]{1,0:T(8,128)(2,1)S(1)}, bf16[400,512]{1,0:T(8,128)(2,1)S(1)}, u32[]{:S(2)}, u32[]{:S(2)}) collective-permute-start(bf16[400,512]{1,0:T(8,128)(2,1)S(1)} %get-tuple-element.70), channel_id=1, source_target_pairs={{0,6},{1,7},{2,4},{3,5},{4,2},{5,3},{6,0},{7,1},{8,14},{9,15},{10,... | collective-permute-start | bytes 1228808 | tf_op jit(solution)/shard_map/ppermute | solution.py:19
  33.5 3.9 %collective-permute-done.6.got2 = bf16[400,512]{1,0:T(8,128)(2,1)S(1)} collective-permute-done((bf16[400,512]{1,0:T(8,128)(2,1)S(1)}, bf16[400,512]{1,0:T(8,128)(2,1)S(1)}, u32[]{:S(2)}, u32[]{:S(2)}) %collective-permute-start.6) | collective-permute-done | bytes 409632 | tf_op jit(solution)/shard_map/ppermute | solution.py:24
  37.3 0.4 collective-permute-start.10
  37.7 1.7 %collective-permute-done.7.got3 = bf16[400,512]{1,0:T(8,128)(2,1)S(1)} collective-permute-done((bf16[400,512]{1,0:T(8,128)(2,1)S(1)}, bf16[400,512]{1,0:T(8,128)(2,1)S(1)}, u32[]{:S(2)}, u32[]{:S(2)}) %collective-permute-start.7) | collective-permute-done | bytes 409632 | tf_op jit(solution)/shard_map/ppermute | solution.py:24
  39.4 2.4 %act_second.1 = (bf16[400,512]{1,0:T(8,128)(2,1)S(1)}, f32[384,512]{1,0:T(8,128)S(1)}) custom-call(s32[4]{0:T(128)S(1)} %pad_add_fusion.place, f32[384,512]{1,0:T(8,128)S(1)} %get-tuple-element.47.keep, bf16[400,512]{1,0:T(8,128)(2,1)S(1)} %collective-permute-done.5.got1, bf16[400,512]{1,0:T(8,128)(2,1)S(1)} %collective-permute-done.6.got2, ...), custom_call_target="tpu_custom_call" | custom-call | bytes 3211264 | tf_op jit(solution)/shard_map/act_second/pallas_call | solution.py:68
  41.9 7.0 %collective-permute-start.15 = (bf16[400,512]{1,0:T(8,128)(2,1)S(1)}, bf16[400,512]{1,0:T(8,128)(2,1)S(1)}, u32[]{:S(2)}, u32[]{:S(2)}) collective-permute-start(bf16[400,512]{1,0:T(8,128)(2,1)S(1)} %get-tuple-element.77), channel_id=1, source_target_pairs={{0,32},{32,0},{64,96},{96,64},{128,160},{160,128},{192,224},{224,1... | collective-permute-start | bytes 1228808 | tf_op jit(solution)/shard_map/ppermute | solution.py:24
  48.9 1.6 %grad_z0.1 = (bf16[112,512]{1,0:T(8,128)(2,1)S(1)}, bf16[112,512]{1,0:T(8,128)(2,1)S(1)}, bf16[112,512]{1,0:T(8,128)(2,1)S(1)}, f32[96,512]{1,0:T(8,128)S(1)}) custom-call(s32[4]{0:T(128)S(1)} %pad_add_fusion.place, f32[384,1024]{1,0:T(8,128)S(1)} %get-tuple-element.53.p0, bf16[400,512]{1,0:T(8,128)(2,1)S(1)} %collective-permute-done.8.got_p, ...), custom_call_target="tpu_custom_call" | custom-call | bytes 2932736 | tf_op jit(solution)/shard_map/grad_z0/pallas_call | solution.py:68
  50.5 0.8 collective-permute-start.12
  51.3 1.2 collective-permute-start.13
  52.5 1.6 %collective-permute-start.14 = (bf16[112,512]{1,0:T(8,128)(2,1)S(1)}, bf16[112,512]{1,0:T(8,128)(2,1)S(1)}, u32[]{:S(2)}, u32[]{:S(2)}) collective-permute-start(bf16[112,512]{1,0:T(8,128)(2,1)S(1)} %get-tuple-element.75), channel_id=1, source_target_pairs={{0,24},{1,25},{2,26},{3,27},{4,28},{5,29},{6,30},{7,31},{8,16},{9,... | collective-permute-start | bytes 344072 | tf_op jit(solution)/shard_map/ppermute | solution.py:19
  54.1 1.6 %grad_z1.1 = (bf16[112,512]{1,0:T(8,128)(2,1)S(1)}, bf16[112,512]{1,0:T(8,128)(2,1)S(1)}, bf16[112,512]{1,0:T(8,128)(2,1)S(1)}, f32[96,512]{1,0:T(8,128)S(1)}) custom-call(s32[4]{0:T(128)S(1)} %pad_add_fusion.place, f32[384,1024]{1,0:T(8,128)S(1)} %get-tuple-element.53.p0, bf16[400,512]{1,0:T(8,128)(2,1)S(1)} %collective-permute-done.10.got_p, ...), custom_call_target="tpu_custom_call" | custom-call | bytes 2932736 | tf_op jit(solution)/shard_map/grad_z1/pallas_call | solution.py:68
  55.9 14.6 %collective-permute-done.12.got1 = bf16[112,512]{1,0:T(8,128)(2,1)S(1)} collective-permute-done((bf16[112,512]{1,0:T(8,128)(2,1)S(1)}, bf16[112,512]{1,0:T(8,128)(2,1)S(1)}, u32[]{:S(2)}, u32[]{:S(2)}) %collective-permute-start.12) | collective-permute-done | bytes 114720 | tf_op jit(solution)/shard_map/ppermute | solution.py:19
  70.5 1.5 %collective-permute-start.17 = (bf16[112,512]{1,0:T(8,128)(2,1)S(1)}, bf16[112,512]{1,0:T(8,128)(2,1)S(1)}, u32[]{:S(2)}, u32[]{:S(2)}) collective-permute-start(bf16[112,512]{1,0:T(8,128)(2,1)S(1)} %get-tuple-element.80), channel_id=1, source_target_pairs={{0,16},{1,17},{2,18},{3,19},{4,20},{5,21},{6,22},{7,23},{8,24},{9,... | collective-permute-start | bytes 344072 | tf_op jit(solution)/shard_map/ppermute | solution.py:19
  72.0 0.1 collective-permute-done.13.got2
  72.1 3.0 %collective-permute-start.18 = (bf16[112,512]{1,0:T(8,128)(2,1)S(1)}, bf16[112,512]{1,0:T(8,128)(2,1)S(1)}, u32[]{:S(2)}, u32[]{:S(2)}) collective-permute-start(bf16[112,512]{1,0:T(8,128)(2,1)S(1)} %get-tuple-element.81), channel_id=1, source_target_pairs={{0,24},{1,25},{2,26},{3,27},{4,28},{5,29},{6,30},{7,31},{8,16},{9,... | collective-permute-start | bytes 344072 | tf_op jit(solution)/shard_map/ppermute | solution.py:19
  75.1 0.8 grad_round0.1.g0
  75.9 0.4 collective-permute-start.21
  76.3 1.0 act_round.1.a0
  77.3 0.3 collective-permute-start.24
  77.6 0.5 collective-permute-start.23
  78.1 9.3 %collective-permute-done.17.got2 = bf16[112,512]{1,0:T(8,128)(2,1)S(1)} collective-permute-done((bf16[112,512]{1,0:T(8,128)(2,1)S(1)}, bf16[112,512]{1,0:T(8,128)(2,1)S(1)}, u32[]{:S(2)}, u32[]{:S(2)}) %collective-permute-start.17) | collective-permute-done | bytes 114720 | tf_op jit(solution)/shard_map/ppermute | solution.py:19
  87.5 3.6 %collective-permute-start.20 = (bf16[96,512]{1,0:T(8,128)(2,1)S(1)}, bf16[96,512]{1,0:T(8,128)(2,1)S(1)}, u32[]{:S(2)}, u32[]{:S(2)}) collective-permute-start(bf16[96,512]{1,0:T(8,128)(2,1)S(1)} %grad_round0.1.g0), channel_id=1, source_target_pairs={{0,16},{1,17},{2,18},{3,19},{4,20},{5,21},{6,22},{7,23},{8,24},{9,... | collective-permute-start | bytes 294920 | tf_op jit(solution)/shard_map/ppermute | solution.py:19
  91.1 1.2 collective-permute-start.19
  92.3 0.8 grad_round1.1.g0
  93.1 0.2 collective-permute-done.20.g2
  93.4 2.5 %collective-permute-done.19.g1 = bf16[96,512]{1,0:T(8,128)(2,1)S(1)} collective-permute-done((bf16[96,512]{1,0:T(8,128)(2,1)S(1)}, bf16[96,512]{1,0:T(8,128)(2,1)S(1)}, u32[]{:S(2)}, u32[]{:S(2)}) %collective-permute-start.19) | collective-permute-done | bytes 98336 | tf_op jit(solution)/shard_map/ppermute | solution.py:19
  95.9 0.6 grad_join0.1.g
  96.4 0.9 collective-permute-start.26
  97.3 3.2 %collective-permute-start.32 = (bf16[96,512]{1,0:T(8,128)(2,1)S(1)}, bf16[96,512]{1,0:T(8,128)(2,1)S(1)}, u32[]{:S(2)}, u32[]{:S(2)}) collective-permute-start(bf16[96,512]{1,0:T(8,128)(2,1)S(1)} %grad_round1.1.g0), channel_id=1, source_target_pairs={{0,24},{1,25},{2,26},{3,27},{4,28},{5,29},{6,30},{7,31},{8,16},{9,... | collective-permute-start | bytes 294920 | tf_op jit(solution)/shard_map/ppermute | solution.py:19
  100.5 5.0 %collective-permute-start.31 = (bf16[96,512]{1,0:T(8,128)(2,1)S(1)}, bf16[96,512]{1,0:T(8,128)(2,1)S(1)}, u32[]{:S(2)}, u32[]{:S(2)}) collective-permute-start(bf16[96,512]{1,0:T(8,128)(2,1)S(1)} %grad_round1.1.g0), channel_id=1, source_target_pairs={{0,16},{1,17},{2,18},{3,19},{4,20},{5,21},{6,22},{7,23},{8,24},{9,... | collective-permute-start | bytes 294920 | tf_op jit(solution)/shard_map/ppermute | solution.py:19
  105.5 0.6 act_join.1.acts
  106.2 5.5 %collective-permute-done.31.g2 = bf16[96,512]{1,0:T(8,128)(2,1)S(1)} collective-permute-done((bf16[96,512]{1,0:T(8,128)(2,1)S(1)}, bf16[96,512]{1,0:T(8,128)(2,1)S(1)}, u32[]{:S(2)}, u32[]{:S(2)}) %collective-permute-start.31) | collective-permute-done | bytes 98336 | tf_op jit(solution)/shard_map/ppermute | solution.py:19
  111.7 0.6 grad_join1.1.g
  112.3 0.9 collective-permute-start.34
  113.2 1.8 %collective-permute-start.33 = (bf16[2,384,256]{2,1,0:T(8,128)(2,1)S(1)}, bf16[2,384,256]{2,1,0:T(8,128)(2,1)S(1)}, u32[]{:S(2)}, u32[]{:S(2)}) collective-permute-start(bf16[2,384,256]{2,1,0:T(8,128)(2,1)S(1)} %grad_join1.1.g), channel_id=1, source_target_pairs={{0,2},{1,3},{2,0},{3,1},{4,6},{5,7},{6,4},{7,5},{8,10},{9,11},{10,... | collective-permute-start | bytes 1179656 | tf_op jit(solution)/shard_map/ppermute | solution.py:19
  115.1 1.6 %collective-permute-start.27 = (bf16[384,256]{1,0:T(8,128)(2,1)S(1)}, bf16[384,256]{1,0:T(8,128)(2,1)S(1)}, u32[]{:S(2)}, u32[]{:S(2)}) collective-permute-start(bf16[384,256]{1,0:T(8,128)(2,1)S(1)} %slice_bitcast_fusion.3), channel_id=1, source_target_pairs={{0,6},{1,7},{2,4},{3,5},{4,2},{5,3},{6,0},{7,1},{8,14},{9,15},{10,... | collective-permute-start | bytes 589832 | tf_op jit(solution)/shard_map/ppermute | solution.py:19
  116.7 5.7 %collective-permute-done.34.g_q = bf16[2,384,256]{2,1,0:T(8,128)(2,1)S(1)} collective-permute-done((bf16[2,384,256]{2,1,0:T(8,128)(2,1)S(1)}, bf16[2,384,256]{2,1,0:T(8,128)(2,1)S(1)}, u32[]{:S(2)}, u32[]{:S(2)}) %collective-permute-start.34) | collective-permute-done | bytes 393248 | tf_op jit(solution)/shard_map/ppermute | solution.py:19
  122.4 0.8 collective-permute-start.36
  123.2 2.8 %collective-permute-start.35 = (bf16[384,256]{1,0:T(8,128)(2,1)S(1)}, bf16[384,256]{1,0:T(8,128)(2,1)S(1)}, u32[]{:S(2)}, u32[]{:S(2)}) collective-permute-start(bf16[384,256]{1,0:T(8,128)(2,1)S(1)} %slice_bitcast_fusion.1), channel_id=1, source_target_pairs={{0,6},{1,7},{2,4},{3,5},{4,2},{5,3},{6,0},{7,1},{8,14},{9,15},{10,... | collective-permute-start | bytes 589832 | tf_op jit(solution)/shard_map/ppermute | solution.py:19
  126.0 0.9 collective-permute-done.28.far_b
  126.9 1.6 %square0.1 = (f32[512,256]{1,0:T(8,128)S(1)}, f32[512,256]{1,0:T(8,128)S(1)}) custom-call(s32[4]{0:T(128)S(1)} %pad_add_fusion.place, bf16[3,512,512]{2,1,0:T(8,128)(2,1)S(1)} %act_join.1.acts, bf16[2,384,256]{2,1,0:T(8,128)(2,1)S(1)} %grad_join0.1.g, bf16[2,384,256]{2,1,0:T(8,128)(2,1)S(1)} %collective-permute-done.25.g_p, ...), custom_call_target="tpu_custom_call" | custom-call | flops 805306368 | bytes 4194304 | tf_op jit(solution)/shard_map/square0/pallas_call | solution.py:68
  128.5 4.6 %collective-permute-start.29 = (f32[512,256]{1,0:T(8,128)S(1)}, f32[512,256]{1,0:T(8,128)S(1)}, u32[]{:S(2)}, u32[]{:S(2)}) collective-permute-start(f32[512,256]{1,0:T(8,128)S(1)} %get-tuple-element.85), channel_id=1, source_target_pairs={{0,1},{1,0},{2,3},{3,2},{4,5},{5,4},{6,7},{7,6},{8,9},{9,8},{10,11... | collective-permute-start | bytes 1572872 | tf_op jit(solution)/shard_map/ppermute | solution.py:19
  133.1 1.6 %square1.1 = (f32[512,256]{1,0:T(8,128)S(1)}, f32[512,256]{1,0:T(8,128)S(1)}) custom-call(s32[4]{0:T(128)S(1)} %pad_add_fusion.place, bf16[3,512,512]{2,1,0:T(8,128)(2,1)S(1)} %act_join.1.acts, bf16[2,384,256]{2,1,0:T(8,128)(2,1)S(1)} %grad_join1.1.g, bf16[2,384,256]{2,1,0:T(8,128)(2,1)S(1)} %collective-permute-done.33.g_p, ...), custom_call_target="tpu_custom_call" | custom-call | flops 805306368 | bytes 4194304 | tf_op jit(solution)/shard_map/square1/pallas_call | solution.py:68
  134.7 1.4 collective-permute-start.37
  136.0 1.5 %collective-permute-done.37.refs_3_ = f32[512,256]{1,0:T(8,128)S(1)} collective-permute-done((f32[512,256]{1,0:T(8,128)S(1)}, f32[512,256]{1,0:T(8,128)S(1)}, u32[]{:S(2)}, u32[]{:S(2)}) %collective-permute-start.37) | collective-permute-done | bytes 524320 | tf_op jit(solution)/shard_map/ppermute | solution.py:19
  137.6 1.6 %mean.1 = f32[1024,256]{1,0:T(8,128)} custom-call(s32[4]{0:T(128)S(1)} %pad_add_fusion.place, f32[512,256]{1,0:T(8,128)S(1)} %get-tuple-element.84.refs_0_, f32[512,256]{1,0:T(8,128)S(1)} %collective-permute-done.29.refs_1_, f32[512,256]{1,0:T(8,128)S(1)} %get-tuple-element.87.refs_2_, f32[512,256]{1,0:T(8,128)S(1)} %collective-permute-done.37.refs_3_), custom_call_target="tpu_custom_call" | custom-call | bytes 3145728 | tf_op jit(solution)/shard_map/mean/pallas_call | solution.py:68
  (42 shorter events, 0.5 us)
Async XLA Ops:
  0.0 5.0 %collective-permute-start = (bf16[1024,256]{1,0:T(8,128)(2,1)}, bf16[1024,256]{1,0:T(8,128)(2,1)S(1)}, u32[]{:S(2)}, u32[]{:S(2)}) collective-permute-start(bf16[1024,256]{1,0:T(8,128)(2,1)} %ab_own.1), channel_id=1, source_target_pairs={{0,1},{1,0},{2,3},{3,2},{4,5},{5,4},{6,7},{7,6},{8,9},{9,8},{10,11... | collective-permute-start | bytes 1572872 | tf_op jit(solution)/shard_map/ppermute | solution.py:19
  5.0 7.8 %collective-permute-start.1 = (bf16[3072,256]{1,0:T(8,128)(2,1)}, bf16[3072,256]{1,0:T(8,128)(2,1)S(1)}, u32[]{:S(2)}, u32[]{:S(2)}) collective-permute-start(bf16[3072,256]{1,0:T(8,128)(2,1)} %own.3), channel_id=1, source_target_pairs={{0,1},{1,0},{2,3},{3,2},{4,5},{5,4},{6,7},{7,6},{8,9},{9,8},{10,11... | collective-permute-start | bytes 4718600 | tf_op jit(solution)/shard_map/ppermute | solution.py:19
  5.4 7.5 %collective-permute-start.2 = (bf16[256,1024]{1,0:T(8,128)(2,1)}, bf16[256,1024]{1,0:T(8,128)(2,1)S(1)}, u32[]{:S(2)}, u32[]{:S(2)}) collective-permute-start(bf16[256,1024]{1,0:T(8,128)(2,1)} %gb_own.3), channel_id=1, source_target_pairs={{0,1},{1,0},{2,3},{3,2},{4,5},{5,4},{6,7},{7,6},{8,9},{9,8},{10,11... | collective-permute-start | bytes 1572872 | tf_op jit(solution)/shard_map/ppermute | solution.py:19
  5.6 2.8 %copy-start = (bf16[3072,1024]{1,0:T(8,128)(2,1)S(1)}, bf16[3072,1024]{1,0:T(8,128)(2,1)}, u32[]{:S(2)}) copy-start(bf16[3072,1024]{1,0:T(8,128)(2,1)} %acts.1) | copy-start | bytes 18874372
  8.4 1.0 copy-start.3
  9.4 3.4 %copy-start.1 = (bf16[3072,256]{1,0:T(8,128)(2,1)S(1)}, bf16[3072,256]{1,0:T(8,128)(2,1)}, u32[]{:S(2)}) copy-start(bf16[3072,256]{1,0:T(8,128)(2,1)} %own.3) | copy-start | bytes 4718596
  9.4 3.4 %copy-start.2 = (bf16[256,1024]{1,0:T(8,128)(2,1)S(1)}, bf16[256,1024]{1,0:T(8,128)(2,1)}, u32[]{:S(2)}) copy-start(bf16[256,1024]{1,0:T(8,128)(2,1)} %gb_own.3) | copy-start | bytes 1572868
  14.7 10.8 %collective-permute-start.4 = (bf16[400,512]{1,0:T(8,128)(2,1)S(1)}, bf16[400,512]{1,0:T(8,128)(2,1)S(1)}, u32[]{:S(2)}, u32[]{:S(2)}) collective-permute-start(bf16[400,512]{1,0:T(8,128)(2,1)S(1)} %get-tuple-element.57), channel_id=1, source_target_pairs={{0,2},{1,3},{2,0},{3,1},{4,6},{5,7},{6,4},{7,5},{8,10},{9,11},{10,... | collective-permute-start | bytes 1228808 | tf_op jit(solution)/shard_map/ppermute | solution.py:19
  14.8 12.0 %collective-permute-start.3 = (bf16[400,512]{1,0:T(8,128)(2,1)S(1)}, bf16[400,512]{1,0:T(8,128)(2,1)S(1)}, u32[]{:S(2)}, u32[]{:S(2)}) collective-permute-start(bf16[400,512]{1,0:T(8,128)(2,1)S(1)} %get-tuple-element.51), channel_id=1, source_target_pairs={{0,6},{1,7},{2,4},{3,5},{4,2},{5,3},{6,0},{7,1},{8,14},{9,15},{10,... | collective-permute-start | bytes 1228808 | tf_op jit(solution)/shard_map/ppermute | solution.py:19
  16.3 15.2 %collective-permute-start.5 = (bf16[400,512]{1,0:T(8,128)(2,1)S(1)}, bf16[400,512]{1,0:T(8,128)(2,1)S(1)}, u32[]{:S(2)}, u32[]{:S(2)}) collective-permute-start(bf16[400,512]{1,0:T(8,128)(2,1)S(1)} %get-tuple-element.62), channel_id=1, source_target_pairs={{0,64},{32,96},{64,0},{96,32},{128,192},{160,224},{192,128},{224,1... | collective-permute-start | bytes 1228808 | tf_op jit(solution)/shard_map/ppermute | solution.py:24
  17.5 19.8 %collective-permute-start.6 = (bf16[400,512]{1,0:T(8,128)(2,1)S(1)}, bf16[400,512]{1,0:T(8,128)(2,1)S(1)}, u32[]{:S(2)}, u32[]{:S(2)}) collective-permute-start(bf16[400,512]{1,0:T(8,128)(2,1)S(1)} %get-tuple-element.63), channel_id=1, source_target_pairs={{0,128},{32,160},{64,192},{96,224},{128,0},{160,32},{192,64},{224,... | collective-permute-start | bytes 1228808 | tf_op jit(solution)/shard_map/ppermute | solution.py:24
  19.9 19.5 %collective-permute-start.7 = (bf16[400,512]{1,0:T(8,128)(2,1)S(1)}, bf16[400,512]{1,0:T(8,128)(2,1)S(1)}, u32[]{:S(2)}, u32[]{:S(2)}) collective-permute-start(bf16[400,512]{1,0:T(8,128)(2,1)S(1)} %get-tuple-element.64), channel_id=1, source_target_pairs={{0,192},{32,224},{64,128},{96,160},{128,64},{160,96},{192,0},{224,... | collective-permute-start | bytes 1228808 | tf_op jit(solution)/shard_map/ppermute | solution.py:24
  28.6 20.2 %collective-permute-start.9 = (bf16[400,512]{1,0:T(8,128)(2,1)S(1)}, bf16[400,512]{1,0:T(8,128)(2,1)S(1)}, u32[]{:S(2)}, u32[]{:S(2)}) collective-permute-start(bf16[400,512]{1,0:T(8,128)(2,1)S(1)} %get-tuple-element.67), channel_id=1, source_target_pairs={{0,6},{1,7},{2,4},{3,5},{4,2},{5,3},{6,0},{7,1},{8,14},{9,15},{10,... | collective-permute-start | bytes 1228808 | tf_op jit(solution)/shard_map/ppermute | solution.py:19
  29.7 19.1 %collective-permute-start.8 = (bf16[400,512]{1,0:T(8,128)(2,1)S(1)}, bf16[400,512]{1,0:T(8,128)(2,1)S(1)}, u32[]{:S(2)}, u32[]{:S(2)}) collective-permute-start(bf16[400,512]{1,0:T(8,128)(2,1)S(1)} %get-tuple-element.58), channel_id=1, source_target_pairs={{0,2},{1,3},{2,0},{3,1},{4,6},{5,7},{6,4},{7,5},{8,10},{9,11},{10,... | collective-permute-start | bytes 1228808 | tf_op jit(solution)/shard_map/ppermute | solution.py:19
  31.5 21.0 %collective-permute-start.11 = (bf16[400,512]{1,0:T(8,128)(2,1)S(1)}, bf16[400,512]{1,0:T(8,128)(2,1)S(1)}, u32[]{:S(2)}, u32[]{:S(2)}) collective-permute-start(bf16[400,512]{1,0:T(8,128)(2,1)S(1)} %get-tuple-element.70), channel_id=1, source_target_pairs={{0,6},{1,7},{2,4},{3,5},{4,2},{5,3},{6,0},{7,1},{8,14},{9,15},{10,... | collective-permute-start | bytes 1228808 | tf_op jit(solution)/shard_map/ppermute | solution.py:19
  37.3 16.8 %collective-permute-start.10 = (bf16[400,512]{1,0:T(8,128)(2,1)S(1)}, bf16[400,512]{1,0:T(8,128)(2,1)S(1)}, u32[]{:S(2)}, u32[]{:S(2)}) collective-permute-start(bf16[400,512]{1,0:T(8,128)(2,1)S(1)} %get-tuple-element.60), channel_id=1, source_target_pairs={{0,2},{1,3},{2,0},{3,1},{4,6},{5,7},{6,4},{7,5},{8,10},{9,11},{10,... | collective-permute-start | bytes 1228808 | tf_op jit(solution)/shard_map/ppermute | solution.py:19
  41.9 34.4 %collective-permute-start.15 = (bf16[400,512]{1,0:T(8,128)(2,1)S(1)}, bf16[400,512]{1,0:T(8,128)(2,1)S(1)}, u32[]{:S(2)}, u32[]{:S(2)}) collective-permute-start(bf16[400,512]{1,0:T(8,128)(2,1)S(1)} %get-tuple-element.77), channel_id=1, source_target_pairs={{0,32},{32,0},{64,96},{96,64},{128,160},{160,128},{192,224},{224,1... | collective-permute-start | bytes 1228808 | tf_op jit(solution)/shard_map/ppermute | solution.py:24
  50.5 20.0 %collective-permute-start.12 = (bf16[112,512]{1,0:T(8,128)(2,1)S(1)}, bf16[112,512]{1,0:T(8,128)(2,1)S(1)}, u32[]{:S(2)}, u32[]{:S(2)}) collective-permute-start(bf16[112,512]{1,0:T(8,128)(2,1)S(1)} %get-tuple-element.73), channel_id=1, source_target_pairs={{0,8},{1,9},{2,10},{3,11},{4,12},{5,13},{6,14},{7,15},{8,0},{9,1},... | collective-permute-start | bytes 344072 | tf_op jit(solution)/shard_map/ppermute | solution.py:19
  51.3 20.8 %collective-permute-start.13 = (bf16[112,512]{1,0:T(8,128)(2,1)S(1)}, bf16[112,512]{1,0:T(8,128)(2,1)S(1)}, u32[]{:S(2)}, u32[]{:S(2)}) collective-permute-start(bf16[112,512]{1,0:T(8,128)(2,1)S(1)} %get-tuple-element.74), channel_id=1, source_target_pairs={{0,16},{1,17},{2,18},{3,19},{4,20},{5,21},{6,22},{7,23},{8,24},{9,... | collective-permute-start | bytes 344072 | tf_op jit(solution)/shard_map/ppermute | solution.py:19
  52.5 22.6 %collective-permute-start.14 = (bf16[112,512]{1,0:T(8,128)(2,1)S(1)}, bf16[112,512]{1,0:T(8,128)(2,1)S(1)}, u32[]{:S(2)}, u32[]{:S(2)}) collective-permute-start(bf16[112,512]{1,0:T(8,128)(2,1)S(1)} %get-tuple-element.75), channel_id=1, source_target_pairs={{0,24},{1,25},{2,26},{3,27},{4,28},{5,29},{6,30},{7,31},{8,16},{9,... | collective-permute-start | bytes 344072 | tf_op jit(solution)/shard_map/ppermute | solution.py:19
  55.8 21.8 %collective-permute-start.16 = (bf16[112,512]{1,0:T(8,128)(2,1)S(1)}, bf16[112,512]{1,0:T(8,128)(2,1)S(1)}, u32[]{:S(2)}, u32[]{:S(2)}) collective-permute-start(bf16[112,512]{1,0:T(8,128)(2,1)S(1)} %get-tuple-element.79), channel_id=1, source_target_pairs={{0,8},{1,9},{2,10},{3,11},{4,12},{5,13},{6,14},{7,15},{8,0},{9,1},... | collective-permute-start | bytes 344072 | tf_op jit(solution)/shard_map/ppermute | solution.py:19
  70.5 17.0 %collective-permute-start.17 = (bf16[112,512]{1,0:T(8,128)(2,1)S(1)}, bf16[112,512]{1,0:T(8,128)(2,1)S(1)}, u32[]{:S(2)}, u32[]{:S(2)}) collective-permute-start(bf16[112,512]{1,0:T(8,128)(2,1)S(1)} %get-tuple-element.80), channel_id=1, source_target_pairs={{0,16},{1,17},{2,18},{3,19},{4,20},{5,21},{6,22},{7,23},{8,24},{9,... | collective-permute-start | bytes 344072 | tf_op jit(solution)/shard_map/ppermute | solution.py:19
  72.1 15.3 %collective-permute-start.18 = (bf16[112,512]{1,0:T(8,128)(2,1)S(1)}, bf16[112,512]{1,0:T(8,128)(2,1)S(1)}, u32[]{:S(2)}, u32[]{:S(2)}) collective-permute-start(bf16[112,512]{1,0:T(8,128)(2,1)S(1)} %get-tuple-element.81), channel_id=1, source_target_pairs={{0,24},{1,25},{2,26},{3,27},{4,28},{5,29},{6,30},{7,31},{8,16},{9,... | collective-permute-start | bytes 344072 | tf_op jit(solution)/shard_map/ppermute | solution.py:19
  75.9 15.1 %collective-permute-start.21 = (bf16[96,512]{1,0:T(8,128)(2,1)S(1)}, bf16[96,512]{1,0:T(8,128)(2,1)S(1)}, u32[]{:S(2)}, u32[]{:S(2)}) collective-permute-start(bf16[96,512]{1,0:T(8,128)(2,1)S(1)} %grad_round0.1.g0), channel_id=1, source_target_pairs={{0,24},{1,25},{2,26},{3,27},{4,28},{5,29},{6,30},{7,31},{8,16},{9,... | collective-permute-start | bytes 294920 | tf_op jit(solution)/shard_map/ppermute | solution.py:19
  77.3 20.0 %collective-permute-start.24 = (bf16[384,512]{1,0:T(8,128)(2,1)S(1)}, bf16[384,512]{1,0:T(8,128)(2,1)S(1)}, u32[]{:S(2)}, u32[]{:S(2)}) collective-permute-start(bf16[384,512]{1,0:T(8,128)(2,1)S(1)} %act_round.1.a0), channel_id=1, source_target_pairs={{0,192},{32,224},{64,128},{96,160},{128,64},{160,96},{192,0},{224,... | collective-permute-start | bytes 1179656 | tf_op jit(solution)/shard_map/ppermute | solution.py:24
  77.6 22.9 %collective-permute-start.23 = (bf16[384,512]{1,0:T(8,128)(2,1)S(1)}, bf16[384,512]{1,0:T(8,128)(2,1)S(1)}, u32[]{:S(2)}, u32[]{:S(2)}) collective-permute-start(bf16[384,512]{1,0:T(8,128)(2,1)S(1)} %act_round.1.a0), channel_id=1, source_target_pairs={{0,128},{32,160},{64,192},{96,224},{128,0},{160,32},{192,64},{224,... | collective-permute-start | bytes 1179656 | tf_op jit(solution)/shard_map/ppermute | solution.py:24
  87.5 18.1 %collective-permute-start.22 = (bf16[384,512]{1,0:T(8,128)(2,1)S(1)}, bf16[384,512]{1,0:T(8,128)(2,1)S(1)}, u32[]{:S(2)}, u32[]{:S(2)}) collective-permute-start(bf16[384,512]{1,0:T(8,128)(2,1)S(1)} %act_round.1.a0), channel_id=1, source_target_pairs={{0,64},{32,96},{64,0},{96,32},{128,192},{160,224},{192,128},{224,1... | collective-permute-start | bytes 1179656 | tf_op jit(solution)/shard_map/ppermute | solution.py:24
  87.5 5.9 %collective-permute-start.20 = (bf16[96,512]{1,0:T(8,128)(2,1)S(1)}, bf16[96,512]{1,0:T(8,128)(2,1)S(1)}, u32[]{:S(2)}, u32[]{:S(2)}) collective-permute-start(bf16[96,512]{1,0:T(8,128)(2,1)S(1)} %grad_round0.1.g0), channel_id=1, source_target_pairs={{0,16},{1,17},{2,18},{3,19},{4,20},{5,21},{6,22},{7,23},{8,24},{9,... | collective-permute-start | bytes 294920 | tf_op jit(solution)/shard_map/ppermute | solution.py:19
  91.1 4.8 %collective-permute-start.19 = (bf16[96,512]{1,0:T(8,128)(2,1)S(1)}, bf16[96,512]{1,0:T(8,128)(2,1)S(1)}, u32[]{:S(2)}, u32[]{:S(2)}) collective-permute-start(bf16[96,512]{1,0:T(8,128)(2,1)S(1)} %grad_round0.1.g0), channel_id=1, source_target_pairs={{0,8},{1,9},{2,10},{3,11},{4,12},{5,13},{6,14},{7,15},{8,0},{9,1},... | collective-permute-start | bytes 294920 | tf_op jit(solution)/shard_map/ppermute | solution.py:19
  96.4 18.5 %collective-permute-start.26 = (bf16[2,384,256]{2,1,0:T(8,128)(2,1)S(1)}, bf16[2,384,256]{2,1,0:T(8,128)(2,1)S(1)}, u32[]{:S(2)}, u32[]{:S(2)}) collective-permute-start(bf16[2,384,256]{2,1,0:T(8,128)(2,1)S(1)} %grad_join0.1.g), channel_id=1, source_target_pairs={{0,6},{1,7},{2,4},{3,5},{4,2},{5,3},{6,0},{7,1},{8,14},{9,15},{10,... | collective-permute-start | bytes 1179656 | tf_op jit(solution)/shard_map/ppermute | solution.py:19
  97.3 17.8 %collective-permute-start.25 = (bf16[2,384,256]{2,1,0:T(8,128)(2,1)S(1)}, bf16[2,384,256]{2,1,0:T(8,128)(2,1)S(1)}, u32[]{:S(2)}, u32[]{:S(2)}) collective-permute-start(bf16[2,384,256]{2,1,0:T(8,128)(2,1)S(1)} %grad_join0.1.g), channel_id=1, source_target_pairs={{0,2},{1,3},{2,0},{3,1},{4,6},{5,7},{6,4},{7,5},{8,10},{9,11},{10,... | collective-permute-start | bytes 1179656 | tf_op jit(solution)/shard_map/ppermute | solution.py:19
  97.3 8.9 %collective-permute-start.32 = (bf16[96,512]{1,0:T(8,128)(2,1)S(1)}, bf16[96,512]{1,0:T(8,128)(2,1)S(1)}, u32[]{:S(2)}, u32[]{:S(2)}) collective-permute-start(bf16[96,512]{1,0:T(8,128)(2,1)S(1)} %grad_round1.1.g0), channel_id=1, source_target_pairs={{0,24},{1,25},{2,26},{3,27},{4,28},{5,29},{6,30},{7,31},{8,16},{9,... | collective-permute-start | bytes 294920 | tf_op jit(solution)/shard_map/ppermute | solution.py:19
  100.5 11.2 %collective-permute-start.31 = (bf16[96,512]{1,0:T(8,128)(2,1)S(1)}, bf16[96,512]{1,0:T(8,128)(2,1)S(1)}, u32[]{:S(2)}, u32[]{:S(2)}) collective-permute-start(bf16[96,512]{1,0:T(8,128)(2,1)S(1)} %grad_round1.1.g0), channel_id=1, source_target_pairs={{0,16},{1,17},{2,18},{3,19},{4,20},{5,21},{6,22},{7,23},{8,24},{9,... | collective-permute-start | bytes 294920 | tf_op jit(solution)/shard_map/ppermute | solution.py:19
  105.5 6.2 %collective-permute-start.30 = (bf16[96,512]{1,0:T(8,128)(2,1)S(1)}, bf16[96,512]{1,0:T(8,128)(2,1)S(1)}, u32[]{:S(2)}, u32[]{:S(2)}) collective-permute-start(bf16[96,512]{1,0:T(8,128)(2,1)S(1)} %grad_round1.1.g0), channel_id=1, source_target_pairs={{0,8},{1,9},{2,10},{3,11},{4,12},{5,13},{6,14},{7,15},{8,0},{9,1},... | collective-permute-start | bytes 294920 | tf_op jit(solution)/shard_map/ppermute | solution.py:19
  112.3 10.1 %collective-permute-start.34 = (bf16[2,384,256]{2,1,0:T(8,128)(2,1)S(1)}, bf16[2,384,256]{2,1,0:T(8,128)(2,1)S(1)}, u32[]{:S(2)}, u32[]{:S(2)}) collective-permute-start(bf16[2,384,256]{2,1,0:T(8,128)(2,1)S(1)} %grad_join1.1.g), channel_id=1, source_target_pairs={{0,6},{1,7},{2,4},{3,5},{4,2},{5,3},{6,0},{7,1},{8,14},{9,15},{10,... | collective-permute-start | bytes 1179656 | tf_op jit(solution)/shard_map/ppermute | solution.py:19
  113.2 10.0 %collective-permute-start.33 = (bf16[2,384,256]{2,1,0:T(8,128)(2,1)S(1)}, bf16[2,384,256]{2,1,0:T(8,128)(2,1)S(1)}, u32[]{:S(2)}, u32[]{:S(2)}) collective-permute-start(bf16[2,384,256]{2,1,0:T(8,128)(2,1)S(1)} %grad_join1.1.g), channel_id=1, source_target_pairs={{0,2},{1,3},{2,0},{3,1},{4,6},{5,7},{6,4},{7,5},{8,10},{9,11},{10,... | collective-permute-start | bytes 1179656 | tf_op jit(solution)/shard_map/ppermute | solution.py:19
  115.0 11.9 %collective-permute-start.28 = (bf16[384,256]{1,0:T(8,128)(2,1)S(1)}, bf16[384,256]{1,0:T(8,128)(2,1)S(1)}, u32[]{:S(2)}, u32[]{:S(2)}) collective-permute-start(bf16[384,256]{1,0:T(8,128)(2,1)S(1)} %slice_bitcast_fusion.2), channel_id=1, source_target_pairs={{0,2},{1,3},{2,0},{3,1},{4,6},{5,7},{6,4},{7,5},{8,10},{9,11},{10,... | collective-permute-start | bytes 589832 | tf_op jit(solution)/shard_map/ppermute | solution.py:19
  115.1 11.7 %collective-permute-start.27 = (bf16[384,256]{1,0:T(8,128)(2,1)S(1)}, bf16[384,256]{1,0:T(8,128)(2,1)S(1)}, u32[]{:S(2)}, u32[]{:S(2)}) collective-permute-start(bf16[384,256]{1,0:T(8,128)(2,1)S(1)} %slice_bitcast_fusion.3), channel_id=1, source_target_pairs={{0,6},{1,7},{2,4},{3,5},{4,2},{5,3},{6,0},{7,1},{8,14},{9,15},{10,... | collective-permute-start | bytes 589832 | tf_op jit(solution)/shard_map/ppermute | solution.py:19
  122.4 10.6 %collective-permute-start.36 = (bf16[384,256]{1,0:T(8,128)(2,1)S(1)}, bf16[384,256]{1,0:T(8,128)(2,1)S(1)}, u32[]{:S(2)}, u32[]{:S(2)}) collective-permute-start(bf16[384,256]{1,0:T(8,128)(2,1)S(1)} %slice_bitcast_fusion), channel_id=1, source_target_pairs={{0,2},{1,3},{2,0},{3,1},{4,6},{5,7},{6,4},{7,5},{8,10},{9,11},{10,... | collective-permute-start | bytes 589832 | tf_op jit(solution)/shard_map/ppermute | solution.py:19
  123.2 9.8 %collective-permute-start.35 = (bf16[384,256]{1,0:T(8,128)(2,1)S(1)}, bf16[384,256]{1,0:T(8,128)(2,1)S(1)}, u32[]{:S(2)}, u32[]{:S(2)}) collective-permute-start(bf16[384,256]{1,0:T(8,128)(2,1)S(1)} %slice_bitcast_fusion.1), channel_id=1, source_target_pairs={{0,6},{1,7},{2,4},{3,5},{4,2},{5,3},{6,0},{7,1},{8,14},{9,15},{10,... | collective-permute-start | bytes 589832 | tf_op jit(solution)/shard_map/ppermute | solution.py:19
  128.5 7.6 %collective-permute-start.29 = (f32[512,256]{1,0:T(8,128)S(1)}, f32[512,256]{1,0:T(8,128)S(1)}, u32[]{:S(2)}, u32[]{:S(2)}) collective-permute-start(f32[512,256]{1,0:T(8,128)S(1)} %get-tuple-element.85), channel_id=1, source_target_pairs={{0,1},{1,0},{2,3},{3,2},{4,5},{5,4},{6,7},{7,6},{8,9},{9,8},{10,11... | collective-permute-start | bytes 1572872 | tf_op jit(solution)/shard_map/ppermute | solution.py:19
  134.7 2.9 %collective-permute-start.37 = (f32[512,256]{1,0:T(8,128)S(1)}, f32[512,256]{1,0:T(8,128)S(1)}, u32[]{:S(2)}, u32[]{:S(2)}) collective-permute-start(f32[512,256]{1,0:T(8,128)S(1)} %get-tuple-element.88), channel_id=1, source_target_pairs={{0,1},{1,0},{2,3},{3,2},{4,5},{5,4},{6,7},{7,6},{8,9},{9,8},{10,11... | collective-permute-start | bytes 1572872 | tf_op jit(solution)/shard_map/ppermute | solution.py:19

commit v2 on v1

--- a/solution.py
+++ b/solution.py
@@ -56,7 +56,7 @@
     return jnp.concatenate(rows, 0)
 
 
-def call(body, place, outs, ins, specs=None, name=None, flops=0, scratch=()):
+def call(body, place, outs, ins, specs=None, name=None, flops=0):
     specs = specs or {}
 
     def whole(shape):
@@ -73,7 +73,6 @@
             grid=(1,),
             in_specs=[specs.get(i) or whole(a.shape) for i, a in enumerate(ins)],
             out_specs=[whole(s) for s, _ in outs],
-            scratch_shapes=scratch,
         ),
         compiler_params=pltpu.CompilerParams(vmem_limit_bytes=24 * 2**20),
         cost_estimate=pl.CostEstimate(flops=flops, bytes_accessed=nbytes, transcendentals=0),
@@ -125,26 +124,37 @@
             out[kind, k * PIECE : (k + 1) * PIECE, :] = ref[:, kind * w : (kind + 1) * w]
 
 
-def act_first(place, acts, ab_own, ab_got, send1, send2, send3, keep):
-    for k, ref in ((1, send1), (2, send2), (3, send3), (0, keep)):
+def act_first(place, acts, ab_own, ab_got, send_a, send_b, keep0, keep1, keep3):
+    w = ab_own.shape[1]
+    for k, ref in ((2, None), (1, keep1), (3, keep3), (0, keep0)):
         rows = quarter_rows(acts, place[1] ^ k)
         v = jnp.concatenate([jnp.dot(rows, ab[...], preferred_element_type=F32) for ab in (ab_own, ab_got)], 1)
-        if k:
-            put(ref, v)
+        if k == 2:
+            put(send_a, v[:, :w])
+            put(send_b, v[:, w:])
         else:
             ref[...] = v
 
 
-def act_second(place, keep, got1, got2, got3, send, total):
-    v = keep[...]
-    for ref in (got1, got2, got3):
-        v = v + get(ref)
+def act_mid(place, keep1, keep3, got_a, got_b, send_p, send_q):
+    w = got_a.shape[1]
+    put(send_p, jnp.concatenate([keep1[:, :w] + get(got_a), keep1[:, w:]], 1))
+    put(send_q, jnp.concatenate([keep3[:, :w], keep3[:, w:] + get(got_b)], 1))
+
+
+def act_second(place, keep, got_p, got_q, total, *sends):
+    v = keep[...] + get(got_p) + get(got_q)
     total[...] = v
-    put(send, v)
-
-
-def act_round(place, total, got, out):
-    out[...] = (total[...] + get(got)).astype(BF16)
+    w = sends[0].shape[1]
+    for i, ref in enumerate(sends):
+        put(ref, v[:, i * w : (i + 1) * w])
+
+
+def act_round(place, total, *refs):
+    out, gots = refs[-1], refs[:-1]
+    w = gots[0].shape[1]
+    for i, got in enumerate(gots):
+        out[:, i * w : (i + 1) * w] = (total[:, i * w : (i + 1) * w] + get(got)).astype(BF16)
 
 
 def act_join(place, a0, a1, a2, a3, out):
@@ -206,16 +216,16 @@
     a_shape = (QUARTER, 2 * cols)
     a_send = ((QUARTER + TAIL, 2 * cols), BF16)
     acts_feats = activations.shape[1]
-    *a_sends, a_keep = call(
+    send_a, send_b, a_keep, a_keep1, a_keep3 = call(
         act_first,
         place,
-        [a_send] * 3 + [(a_shape, F32)],
+        [((QUARTER + TAIL, cols), BF16)] * 2 + [(a_shape, F32)] * 3,
         (activations, act_basis, ab_got),
         {0: core_half(acts_feats)},
         "act_first",
         2 * HALF * acts_feats * 2 * cols,
     )
-    a_got = [row_swap(a, x=k) for k, a in zip((1, 2, 3), a_sends)]
+    a_got_a, a_got_b = row_swap(send_a, x=3), row_swap(send_b, x=1)
 
     grad_ins = (out_grads, og_got, grad_basis, gb_got)
     grad_specs = {0: core_half(feats), 1: core_half(feats)}
@@ -241,8 +251,13 @@
         3 * grad_flops,
     )
 
+    send_p, send_q = call(
+        act_mid, after(place, p1), [a_send] * 2, (a_keep1, a_keep3, a_got_a, a_got_b), None, "act_mid"
+    )
+    a_got_p, a_got_q = row_swap(send_p, x=1), row_swap(send_q, x=3)
+
     got_p, got_q = [], []
-    token = p0
+    token = send_p
     for pair in range(PAIRS):
         wide, narrow = columns((QUARTER, 2 * w), pair), columns((QUARTER + TAIL, w), pair)
         send_p, send_q = call(
@@ -257,10 +272,15 @@
         got_p.append(col_swap(send_p, y=1))
         got_q.append(col_swap(send_q, y=3))
 
-    a_send2, a_total = call(
-        act_second, after(place, token), [a_send, (a_shape, F32)], (a_keep, *a_got), None, "act_second"
-    )
-    a_got2 = row_swap(a_send2, z=1)
+    a_total, *sends = call(
+        act_second,
+        after(place, token),
+        [(a_shape, F32)] + [((QUARTER + TAIL, cols), BF16)] * 2,
+        (a_keep, a_got_p, a_got_q),
+        None,
+        "act_second",
+    )
+    a_got2 = [row_swap(a, z=1) for a in sends]
     token = a_total
 
     keeps, z_gots = [], []
@@ -291,7 +311,7 @@
         g_all.append([g_own, *[col_swap(g_own, z=k) for k in (1, 2, 3)]])
         if pair == 0:
             (a_own,) = call(
-                act_round, after(place, token), [(a_shape, BF16)], (a_total, a_got2), None, "act_round"
+                act_round, after(place, token), [(a_shape, BF16)], (a_total, *a_got2), None, "act_round"
             )
             token = a_own
             a_all = [a_own, *[row_swap(a_own, x=k) for k in (1, 2, 3)]]

time: 139 us -> 131 us (0.942)
  waiting for transfers between devices: 52.5 us -> 34.2 us
  starting transfers between devices: 56.7 us -> 66.9 us
    ppermute x31, waiting for transfers between devices: 46.9 us -> 29.7 us  [col_swap(): return lax.ppermute(a, 'col', perm)]
    ppermute x7 -> x9, starting transfers between devices: 11.6 us -> 18.2 us  [row_swap(): return lax.ppermute(a, 'row', perm)]
    ppermute x31, starting transfers between devices: 45.1 us -> 48.6 us  [col_swap(): return lax.ppermute(a, 'col', perm)]
    ppermute x7 -> x9, waiting for transfers between devices: 5.56 us -> 4.46 us  [row_swap(): return lax.ppermute(a, 'row', perm)]
    pallas_call x17 -> x18, Pallas kernels: 25.7 us -> 25.8 us  [call(): pl.pallas_call(body, out_shape=[jax.ShapeDtypeStruct(s, d) for s, d in ou...]
  transfers between devices with their start and end apart: 38 -> 40, of which waited for: 14 -> 14; matrix products, arithmetic and copies ran while one was open for 0% -> 0% of each run, Pallas kernels for 16% -> 18%
where the time goes in v2:
time: 131 us
  starting transfers between devices  66.9 us (51%)
  waiting for transfers between devices  34.2 us (26%)
  Pallas kernels  25.8 us (20%)
  local copies, waits for them, and re-layouts  3.89 us (3%)
    ppermute x31, starting transfers between devices, col_swap(): return lax.ppermute(a, 'col', perm)  48.6 us
    ppermute x31, waiting for transfers between devices, col_swap(): return lax.ppermute(a, 'col', perm)  29.7 us
    pallas_call x18, Pallas kernels, call(): pl.pallas_call(body, out_shape=[jax.ShapeDtypeStruct(s, d) for s, d in ou...  25.8 us
    ppermute x9, starting transfers between devices, row_swap(): return lax.ppermute(a, 'row', perm)  18.2 us
    ppermute x9, waiting for transfers between devices, row_swap(): return lax.ppermute(a, 'row', perm)  4.46 us
    unnamed x8, local copies, waits for them, and re-layouts  3.83 us
  transfers between devices with their start and end apart: 40, of which 14 were waited for; matrix products, arithmetic and copies ran while one was open for 0% of the time, Pallas kernels for 18%

profile of v2, /device:TPU:1, one launch (start us, length us, event | category | flops | bytes accessed | tf_op | source)
XLA Modules:
  0.0 131.1 jit_solution(17774073367878188326)
XLA Ops:
  0.0 3.2 %collective-permute-start = (bf16[1024,256]{1,0:T(8,128)(2,1)}, bf16[1024,256]{1,0:T(8,128)(2,1)S(1)}, u32[]{:S(2)}, u32[]{:S(2)}) collective-permute-start(bf16[1024,256]{1,0:T(8,128)(2,1)} %ab_own.1), channel_id=1, source_target_pairs={{0,1},{1,0},{2,3},{3,2},{4,5},{5,4},{6,7},{7,6},{8,9},{9,8},{10,11... | collective-permute-start | bytes 1572872 | tf_op jit(solution)/shard_map/ppermute | solution.py:19
  3.2 1.7 %collective-permute-done.ab_got = bf16[1024,256]{1,0:T(8,128)(2,1)S(1)} collective-permute-done((bf16[1024,256]{1,0:T(8,128)(2,1)}, bf16[1024,256]{1,0:T(8,128)(2,1)S(1)}, u32[]{:S(2)}, u32[]{:S(2)}) %collective-permute-start) | collective-permute-done | bytes 524320 | tf_op jit(solution)/shard_map/ppermute | solution.py:19
  5.0 0.4 collective-permute-start.1
  5.6 2.8 %copy-done = bf16[3072,1024]{1,0:T(8,128)(2,1)S(1)} copy-done((bf16[3072,1024]{1,0:T(8,128)(2,1)S(1)}, bf16[3072,1024]{1,0:T(8,128)(2,1)}, u32[]{:S(2)}) %copy-start) | copy-done | bytes 6291480
  8.4 1.0 copy-done.3
  9.4 2.7 %act_first.1 = (bf16[400,256]{1,0:T(8,128)(2,1)S(1)}, bf16[400,256]{1,0:T(8,128)(2,1)S(1)}, f32[384,512]{1,0:T(8,128)S(1)}, f32[384,512]{1,0:T(8,128)S(1)}, f32[384,512]{1,0:T(8,128)S(1)}) custom-call(s32[4]{0:T(128)S(1)} %pad_add_fusion.place, bf16[3072,1024]{1,0:T(8,128)(2,1)S(1)} %copy-done, bf16[1024,256]{1,0:T(8,128)(2,1)S(1)} %copy-done.3, ...), custom_call_target="tpu_custom_call" | custom-call | flops 1610612736 | bytes 10108928 | tf_op jit(solution)/shard_map/act_first/pallas_call | solution.py:68
  12.1 0.8 collective-permute-start.3
  12.9 1.9 %grad_first.1 = (bf16[400,512]{1,0:T(8,128)(2,1)S(1)}, bf16[400,512]{1,0:T(8,128)(2,1)S(1)}) custom-call(s32[4]{0:T(128)S(1)} %pad_add_fusion.place, bf16[3072,256]{1,0:T(8,128)(2,1)S(1)} %copy-done.1, bf16[3072,256]{1,0:T(8,128)(2,1)S(1)} %collective-permute-done.1.got, bf16[256,1024]{1,0:T(8,128)(2,1)S(1)} %copy-done.2, ...), custom_call_target="tpu_custom_call" | custom-call | flops 402653184 | bytes 5013504 | tf_op jit(solution)/shard_map/grad_first/pallas_call | solution.py:68
  14.8 2.8 %collective-permute-start.5 = (bf16[400,512]{1,0:T(8,128)(2,1)S(1)}, bf16[400,512]{1,0:T(8,128)(2,1)S(1)}, u32[]{:S(2)}, u32[]{:S(2)}) collective-permute-start(bf16[400,512]{1,0:T(8,128)(2,1)S(1)} %get-tuple-element.56), channel_id=1, source_target_pairs={{0,6},{1,7},{2,4},{3,5},{4,2},{5,3},{6,0},{7,1},{8,14},{9,15},{10,... | collective-permute-start | bytes 1228808 | tf_op jit(solution)/shard_map/ppermute | solution.py:19
  17.7 1.9 %grad_rest.1 = (f32[384,1024]{1,0:T(8,128)S(1)}, f32[384,1024]{1,0:T(8,128)S(1)}, f32[384,1024]{1,0:T(8,128)S(1)}) custom-call(s32[4]{0:T(128)S(1)} %pad_add_fusion.place, bf16[3072,256]{1,0:T(8,128)(2,1)S(1)} %copy-done.1, bf16[3072,256]{1,0:T(8,128)(2,1)S(1)} %collective-permute-done.1.got, bf16[256,1024]{1,0:T(8,128)(2,1)S(1)} %copy-done.2, ...), custom_call_target="tpu_custom_call" | custom-call | flops 1207959552 | bytes 8912896 | tf_op jit(solution)/shard_map/grad_rest/pallas_call | solution.py:68
  19.7 1.8 %act_mid.1 = (bf16[400,512]{1,0:T(8,128)(2,1)S(1)}, bf16[400,512]{1,0:T(8,128)(2,1)S(1)}) custom-call(s32[4]{0:T(128)S(1)} %pad_add_fusion.place, f32[384,512]{1,0:T(8,128)S(1)} %get-tuple-element.60.keep1, f32[384,512]{1,0:T(8,128)S(1)} %get-tuple-element.61.keep3, bf16[400,256]{1,0:T(8,128)(2,1)S(1)} %collective-permute-done.3.got_a, ...), custom_call_target="tpu_custom_call" | custom-call | bytes 2801664 | tf_op jit(solution)/shard_map/act_mid/pallas_call | solution.py:68
  21.5 1.2 collective-permute-start.8
  23.1 4.4 %collective-permute-done.6.got_b = bf16[400,512]{1,0:T(8,128)(2,1)S(1)} collective-permute-done((bf16[400,512]{1,0:T(8,128)(2,1)S(1)}, bf16[400,512]{1,0:T(8,128)(2,1)S(1)}, u32[]{:S(2)}, u32[]{:S(2)}) %collective-permute-start.6) | collective-permute-done | bytes 409632 | tf_op jit(solution)/shard_map/ppermute | solution.py:19
  27.5 1.8 %grad_second0.1 = (bf16[400,512]{1,0:T(8,128)(2,1)S(1)}, bf16[400,512]{1,0:T(8,128)(2,1)S(1)}) custom-call(s32[4]{0:T(128)S(1)} %pad_add_fusion.place, f32[384,1024]{1,0:T(8,128)S(1)} %get-tuple-element.58.p1, f32[384,1024]{1,0:T(8,128)S(1)} %get-tuple-element.66.p3, bf16[400,512]{1,0:T(8,128)(2,1)S(1)} %collective-permute-done.5.got_a, ...), custom_call_target="tpu_custom_call" | custom-call | bytes 4784128 | tf_op jit(solution)/shard_map/grad_second0/pallas_call | solution.py:68
  29.3 1.6 %collective-permute-start.10 = (bf16[400,512]{1,0:T(8,128)(2,1)S(1)}, bf16[400,512]{1,0:T(8,128)(2,1)S(1)}, u32[]{:S(2)}, u32[]{:S(2)}) collective-permute-start(bf16[400,512]{1,0:T(8,128)(2,1)S(1)} %get-tuple-element.76), channel_id=1, source_target_pairs={{0,6},{1,7},{2,4},{3,5},{4,2},{5,3},{6,0},{7,1},{8,14},{9,15},{10,... | collective-permute-start | bytes 1228808 | tf_op jit(solution)/shard_map/ppermute | solution.py:19
  30.9 1.8 %grad_second1.1 = (bf16[400,512]{1,0:T(8,128)(2,1)S(1)}, bf16[400,512]{1,0:T(8,128)(2,1)S(1)}) custom-call(s32[4]{0:T(128)S(1)} %pad_add_fusion.place, f32[384,1024]{1,0:T(8,128)S(1)} %get-tuple-element.58.p1, f32[384,1024]{1,0:T(8,128)S(1)} %get-tuple-element.66.p3, bf16[400,512]{1,0:T(8,128)(2,1)S(1)} %collective-permute-done.5.got_a, ...), custom_call_target="tpu_custom_call" | custom-call | bytes 4784128 | tf_op jit(solution)/shard_map/grad_second1/pallas_call | solution.py:68
  32.7 1.3 collective-permute-start.12
  33.9 0.9 collective-permute-start.11
  34.8 1.5 %act_second.1 = (f32[384,512]{1,0:T(8,128)S(1)}, bf16[400,256]{1,0:T(8,128)(2,1)S(1)}, bf16[400,256]{1,0:T(8,128)(2,1)S(1)}) custom-call(s32[4]{0:T(128)S(1)} %pad_add_fusion.place, f32[384,512]{1,0:T(8,128)S(1)} %get-tuple-element.52.keep, bf16[400,512]{1,0:T(8,128)(2,1)S(1)} %collective-permute-done.7.got_p, bf16[400,512]{1,0:T(8,128)(2,1)S(1)} %collective-permute-done.8.got_q), custom_call_target="tpu_custom_call" | custom-call | bytes 2801664 | tf_op jit(solution)/shard_map/act_second/pallas_call | solution.py:68
  36.3 7.0 %collective-permute-start.16 = (bf16[400,256]{1,0:T(8,128)(2,1)S(1)}, bf16[400,256]{1,0:T(8,128)(2,1)S(1)}, u32[]{:S(2)}, u32[]{:S(2)}) collective-permute-start(bf16[400,256]{1,0:T(8,128)(2,1)S(1)} %get-tuple-element.86), channel_id=1, source_target_pairs={{0,32},{32,0},{64,96},{96,64},{128,160},{160,128},{192,224},{224,1... | collective-permute-start | bytes 614408 | tf_op jit(solution)/shard_map/ppermute | solution.py:24
  43.3 1.6 %grad_z0.1 = (bf16[112,512]{1,0:T(8,128)(2,1)S(1)}, bf16[112,512]{1,0:T(8,128)(2,1)S(1)}, bf16[112,512]{1,0:T(8,128)(2,1)S(1)}, f32[96,512]{1,0:T(8,128)S(1)}) custom-call(s32[4]{0:T(128)S(1)} %pad_add_fusion.place, f32[384,1024]{1,0:T(8,128)S(1)} %get-tuple-element.75.p0, bf16[400,512]{1,0:T(8,128)(2,1)S(1)} %collective-permute-done.9.got_p, ...), custom_call_target="tpu_custom_call" | custom-call | bytes 2932736 | tf_op jit(solution)/shard_map/grad_z0/pallas_call | solution.py:68
  45.0 0.8 collective-permute-start.13
  45.8 1.2 collective-permute-start.14
  47.0 1.2 collective-permute-done.12.got_q
  48.2 4.3 %collective-permute-start.15 = (bf16[112,512]{1,0:T(8,128)(2,1)S(1)}, bf16[112,512]{1,0:T(8,128)(2,1)S(1)}, u32[]{:S(2)}, u32[]{:S(2)}) collective-permute-start(bf16[112,512]{1,0:T(8,128)(2,1)S(1)} %get-tuple-element.84), channel_id=1, source_target_pairs={{0,24},{1,25},{2,26},{3,27},{4,28},{5,29},{6,30},{7,31},{8,16},{9,... | collective-permute-start | bytes 344072 | tf_op jit(solution)/shard_map/ppermute | solution.py:19
  52.6 4.2 %collective-permute-start.17 = (bf16[400,256]{1,0:T(8,128)(2,1)S(1)}, bf16[400,256]{1,0:T(8,128)(2,1)S(1)}, u32[]{:S(2)}, u32[]{:S(2)}) collective-permute-start(bf16[400,256]{1,0:T(8,128)(2,1)S(1)} %get-tuple-element.87), channel_id=1, source_target_pairs={{0,32},{32,0},{64,96},{96,64},{128,160},{160,128},{192,224},{224,1... | collective-permute-start | bytes 614408 | tf_op jit(solution)/shard_map/ppermute | solution.py:24
  56.8 1.6 %grad_z1.1 = (bf16[112,512]{1,0:T(8,128)(2,1)S(1)}, bf16[112,512]{1,0:T(8,128)(2,1)S(1)}, bf16[112,512]{1,0:T(8,128)(2,1)S(1)}, f32[96,512]{1,0:T(8,128)S(1)}) custom-call(s32[4]{0:T(128)S(1)} %pad_add_fusion.place, f32[384,1024]{1,0:T(8,128)S(1)} %get-tuple-element.75.p0, bf16[400,512]{1,0:T(8,128)(2,1)S(1)} %collective-permute-done.11.got_p, ...), custom_call_target="tpu_custom_call" | custom-call | bytes 2932736 | tf_op jit(solution)/shard_map/grad_z1/pallas_call | solution.py:68
  58.5 1.9 %collective-permute-start.19 = (bf16[112,512]{1,0:T(8,128)(2,1)S(1)}, bf16[112,512]{1,0:T(8,128)(2,1)S(1)}, u32[]{:S(2)}, u32[]{:S(2)}) collective-permute-start(bf16[112,512]{1,0:T(8,128)(2,1)S(1)} %get-tuple-element.90), channel_id=1, source_target_pairs={{0,16},{1,17},{2,18},{3,19},{4,20},{5,21},{6,22},{7,23},{8,24},{9,... | collective-permute-start | bytes 344072 | tf_op jit(solution)/shard_map/ppermute | solution.py:19
  60.4 1.6 %collective-permute-start.20 = (bf16[112,512]{1,0:T(8,128)(2,1)S(1)}, bf16[112,512]{1,0:T(8,128)(2,1)S(1)}, u32[]{:S(2)}, u32[]{:S(2)}) collective-permute-start(bf16[112,512]{1,0:T(8,128)(2,1)S(1)} %get-tuple-element.91), channel_id=1, source_target_pairs={{0,24},{1,25},{2,26},{3,27},{4,28},{5,29},{6,30},{7,31},{8,16},{9,... | collective-permute-start | bytes 344072 | tf_op jit(solution)/shard_map/ppermute | solution.py:19
  62.1 0.8 grad_round0.1.g0
  62.9 1.7 %collective-permute-start.23 = (bf16[96,512]{1,0:T(8,128)(2,1)S(1)}, bf16[96,512]{1,0:T(8,128)(2,1)S(1)}, u32[]{:S(2)}, u32[]{:S(2)}) collective-permute-start(bf16[96,512]{1,0:T(8,128)(2,1)S(1)} %grad_round0.1.g0), channel_id=1, source_target_pairs={{0,24},{1,25},{2,26},{3,27},{4,28},{5,29},{6,30},{7,31},{8,16},{9,... | collective-permute-start | bytes 294920 | tf_op jit(solution)/shard_map/ppermute | solution.py:19
  64.6 4.4 %collective-permute-done.17.refs_1_ = bf16[400,256]{1,0:T(8,128)(2,1)S(1)} collective-permute-done((bf16[400,256]{1,0:T(8,128)(2,1)S(1)}, bf16[400,256]{1,0:T(8,128)(2,1)S(1)}, u32[]{:S(2)}, u32[]{:S(2)}) %collective-permute-start.17) | collective-permute-done | bytes 204832 | tf_op jit(solution)/shard_map/ppermute | solution.py:24
  69.0 1.0 act_round.1.a0
  69.9 0.8 collective-permute-start.26
  70.8 2.4 %collective-permute-start.25 = (bf16[384,512]{1,0:T(8,128)(2,1)S(1)}, bf16[384,512]{1,0:T(8,128)(2,1)S(1)}, u32[]{:S(2)}, u32[]{:S(2)}) collective-permute-start(bf16[384,512]{1,0:T(8,128)(2,1)S(1)} %act_round.1.a0), channel_id=1, source_target_pairs={{0,128},{32,160},{64,192},{96,224},{128,0},{160,32},{192,64},{224,... | collective-permute-start | bytes 1179656 | tf_op jit(solution)/shard_map/ppermute | solution.py:24
  73.2 6.6 %collective-permute-done.19.got2 = bf16[112,512]{1,0:T(8,128)(2,1)S(1)} collective-permute-done((bf16[112,512]{1,0:T(8,128)(2,1)S(1)}, bf16[112,512]{1,0:T(8,128)(2,1)S(1)}, u32[]{:S(2)}, u32[]{:S(2)}) %collective-permute-start.19) | collective-permute-done | bytes 114720 | tf_op jit(solution)/shard_map/ppermute | solution.py:19
  79.8 1.3 %collective-permute-start.24 = (bf16[384,512]{1,0:T(8,128)(2,1)S(1)}, bf16[384,512]{1,0:T(8,128)(2,1)S(1)}, u32[]{:S(2)}, u32[]{:S(2)}) collective-permute-start(bf16[384,512]{1,0:T(8,128)(2,1)S(1)} %act_round.1.a0), channel_id=1, source_target_pairs={{0,64},{32,96},{64,0},{96,32},{128,192},{160,224},{192,128},{224,1... | collective-permute-start | bytes 1179656 | tf_op jit(solution)/shard_map/ppermute | solution.py:24
  81.1 2.9 %collective-permute-start.22 = (bf16[96,512]{1,0:T(8,128)(2,1)S(1)}, bf16[96,512]{1,0:T(8,128)(2,1)S(1)}, u32[]{:S(2)}, u32[]{:S(2)}) collective-permute-start(bf16[96,512]{1,0:T(8,128)(2,1)S(1)} %grad_round0.1.g0), channel_id=1, source_target_pairs={{0,16},{1,17},{2,18},{3,19},{4,20},{5,21},{6,22},{7,23},{8,24},{9,... | collective-permute-start | bytes 294920 | tf_op jit(solution)/shard_map/ppermute | solution.py:19
  84.0 0.9 collective-permute-start.21
  84.9 0.8 grad_round1.1.g0
  85.7 0.8 collective-permute-done.22.g2
  86.5 1.3 collective-permute-done.21.g1
  87.8 0.6 grad_join0.1.g
  88.4 1.7 %collective-permute-start.28 = (bf16[2,384,256]{2,1,0:T(8,128)(2,1)S(1)}, bf16[2,384,256]{2,1,0:T(8,128)(2,1)S(1)}, u32[]{:S(2)}, u32[]{:S(2)}) collective-permute-start(bf16[2,384,256]{2,1,0:T(8,128)(2,1)S(1)} %grad_join0.1.g), channel_id=1, source_target_pairs={{0,6},{1,7},{2,4},{3,5},{4,2},{5,3},{6,0},{7,1},{8,14},{9,15},{10,... | collective-permute-start | bytes 1179656 | tf_op jit(solution)/shard_map/ppermute | solution.py:19
  90.1 0.4 collective-permute-start.27
  90.5 2.8 %collective-permute-start.34 = (bf16[96,512]{1,0:T(8,128)(2,1)S(1)}, bf16[96,512]{1,0:T(8,128)(2,1)S(1)}, u32[]{:S(2)}, u32[]{:S(2)}) collective-permute-start(bf16[96,512]{1,0:T(8,128)(2,1)S(1)} %grad_round1.1.g0), channel_id=1, source_target_pairs={{0,24},{1,25},{2,26},{3,27},{4,28},{5,29},{6,30},{7,31},{8,16},{9,... | collective-permute-start | bytes 294920 | tf_op jit(solution)/shard_map/ppermute | solution.py:19
  93.2 0.8 collective-permute-start.32
  94.0 0.6 act_join.1.acts
  94.7 1.1 collective-permute-done.34.g3
  95.8 2.1 %collective-permute-done.33.g2 = bf16[96,512]{1,0:T(8,128)(2,1)S(1)} collective-permute-done((bf16[96,512]{1,0:T(8,128)(2,1)S(1)}, bf16[96,512]{1,0:T(8,128)(2,1)S(1)}, u32[]{:S(2)}, u32[]{:S(2)}) %collective-permute-start.33) | collective-permute-done | bytes 98336 | tf_op jit(solution)/shard_map/ppermute | solution.py:19
  97.9 0.6 grad_join1.1.g
  98.4 1.6 %collective-permute-start.36 = (bf16[2,384,256]{2,1,0:T(8,128)(2,1)S(1)}, bf16[2,384,256]{2,1,0:T(8,128)(2,1)S(1)}, u32[]{:S(2)}, u32[]{:S(2)}) collective-permute-start(bf16[2,384,256]{2,1,0:T(8,128)(2,1)S(1)} %grad_join1.1.g), channel_id=1, source_target_pairs={{0,6},{1,7},{2,4},{3,5},{4,2},{5,3},{6,0},{7,1},{8,14},{9,15},{10,... | collective-permute-start | bytes 1179656 | tf_op jit(solution)/shard_map/ppermute | solution.py:19
  100.2 1.5 %collective-permute-start.30 = (bf16[384,256]{1,0:T(8,128)(2,1)S(1)}, bf16[384,256]{1,0:T(8,128)(2,1)S(1)}, u32[]{:S(2)}, u32[]{:S(2)}) collective-permute-start(bf16[384,256]{1,0:T(8,128)(2,1)S(1)} %slice_bitcast_fusion.2), channel_id=1, source_target_pairs={{0,2},{1,3},{2,0},{3,1},{4,6},{5,7},{6,4},{7,5},{8,10},{9,11},{10,... | collective-permute-start | bytes 589832 | tf_op jit(solution)/shard_map/ppermute | solution.py:19
  101.6 1.3 collective-permute-start.29
  102.9 5.6 %collective-permute-done.36.g_q = bf16[2,384,256]{2,1,0:T(8,128)(2,1)S(1)} collective-permute-done((bf16[2,384,256]{2,1,0:T(8,128)(2,1)S(1)}, bf16[2,384,256]{2,1,0:T(8,128)(2,1)S(1)}, u32[]{:S(2)}, u32[]{:S(2)}) %collective-permute-start.36) | collective-permute-done | bytes 393248 | tf_op jit(solution)/shard_map/ppermute | solution.py:19
  108.6 1.5 %collective-permute-done.35.g_p = bf16[2,384,256]{2,1,0:T(8,128)(2,1)S(1)} collective-permute-done((bf16[2,384,256]{2,1,0:T(8,128)(2,1)S(1)}, bf16[2,384,256]{2,1,0:T(8,128)(2,1)S(1)}, u32[]{:S(2)}, u32[]{:S(2)}) %collective-permute-start.35) | collective-permute-done | bytes 393248 | tf_op jit(solution)/shard_map/ppermute | solution.py:19
  110.2 1.2 collective-permute-start.37
  111.3 1.8 %collective-permute-done.30.far_b = bf16[384,256]{1,0:T(8,128)(2,1)S(1)} collective-permute-done((bf16[384,256]{1,0:T(8,128)(2,1)S(1)}, bf16[384,256]{1,0:T(8,128)(2,1)S(1)}, u32[]{:S(2)}, u32[]{:S(2)}) %collective-permute-start.30) | collective-permute-done | bytes 196640 | tf_op jit(solution)/shard_map/ppermute | solution.py:19
  113.1 1.6 %square0.1 = (f32[512,256]{1,0:T(8,128)S(1)}, f32[512,256]{1,0:T(8,128)S(1)}) custom-call(s32[4]{0:T(128)S(1)} %pad_add_fusion.place, bf16[3,512,512]{2,1,0:T(8,128)(2,1)S(1)} %act_join.1.acts, bf16[2,384,256]{2,1,0:T(8,128)(2,1)S(1)} %grad_join0.1.g, bf16[2,384,256]{2,1,0:T(8,128)(2,1)S(1)} %collective-permute-done.27.g_p, ...), custom_call_target="tpu_custom_call" | custom-call | flops 805306368 | bytes 4194304 | tf_op jit(solution)/shard_map/square0/pallas_call | solution.py:68
  114.7 8.3 %collective-permute-start.31 = (f32[512,256]{1,0:T(8,128)S(1)}, f32[512,256]{1,0:T(8,128)S(1)}, u32[]{:S(2)}, u32[]{:S(2)}) collective-permute-start(f32[512,256]{1,0:T(8,128)S(1)} %get-tuple-element.95), channel_id=1, source_target_pairs={{0,1},{1,0},{2,3},{3,2},{4,5},{5,4},{6,7},{7,6},{8,9},{9,8},{10,11... | collective-permute-start | bytes 1572872 | tf_op jit(solution)/shard_map/ppermute | solution.py:19
  123.1 1.6 %square1.1 = (f32[512,256]{1,0:T(8,128)S(1)}, f32[512,256]{1,0:T(8,128)S(1)}) custom-call(s32[4]{0:T(128)S(1)} %pad_add_fusion.place, bf16[3,512,512]{2,1,0:T(8,128)(2,1)S(1)} %act_join.1.acts, bf16[2,384,256]{2,1,0:T(8,128)(2,1)S(1)} %grad_join1.1.g, bf16[2,384,256]{2,1,0:T(8,128)(2,1)S(1)} %collective-permute-done.35.g_p, ...), custom_call_target="tpu_custom_call" | custom-call | flops 805306368 | bytes 4194304 | tf_op jit(solution)/shard_map/square1/pallas_call | solution.py:68
  124.7 3.3 %collective-permute-start.39 = (f32[512,256]{1,0:T(8,128)S(1)}, f32[512,256]{1,0:T(8,128)S(1)}, u32[]{:S(2)}, u32[]{:S(2)}) collective-permute-start(f32[512,256]{1,0:T(8,128)S(1)} %get-tuple-element.98), channel_id=1, source_target_pairs={{0,1},{1,0},{2,3},{3,2},{4,5},{5,4},{6,7},{7,6},{8,9},{9,8},{10,11... | collective-permute-start | bytes 1572872 | tf_op jit(solution)/shard_map/ppermute | solution.py:19
  127.9 1.5 %collective-permute-done.39.refs_3_ = f32[512,256]{1,0:T(8,128)S(1)} collective-permute-done((f32[512,256]{1,0:T(8,128)S(1)}, f32[512,256]{1,0:T(8,128)S(1)}, u32[]{:S(2)}, u32[]{:S(2)}) %collective-permute-start.39) | collective-permute-done | bytes 524320 | tf_op jit(solution)/shard_map/ppermute | solution.py:19
  129.5 1.6 %mean.1 = f32[1024,256]{1,0:T(8,128)} custom-call(s32[4]{0:T(128)S(1)} %pad_add_fusion.place, f32[512,256]{1,0:T(8,128)S(1)} %get-tuple-element.94.refs_0_, f32[512,256]{1,0:T(8,128)S(1)} %collective-permute-done.31.refs_1_, f32[512,256]{1,0:T(8,128)S(1)} %get-tuple-element.97.refs_2_, f32[512,256]{1,0:T(8,128)S(1)} %collective-permute-done.39.refs_3_), custom_call_target="tpu_custom_call" | custom-call | bytes 3145728 | tf_op jit(solution)/shard_map/mean/pallas_call | solution.py:68
  (47 shorter events, 1.1 us)
Async XLA Ops:
  0.0 5.0 %collective-permute-start = (bf16[1024,256]{1,0:T(8,128)(2,1)}, bf16[1024,256]{1,0:T(8,128)(2,1)S(1)}, u32[]{:S(2)}, u32[]{:S(2)}) collective-permute-start(bf16[1024,256]{1,0:T(8,128)(2,1)} %ab_own.1), channel_id=1, source_target_pairs={{0,1},{1,0},{2,3},{3,2},{4,5},{5,4},{6,7},{7,6},{8,9},{9,8},{10,11... | collective-permute-start | bytes 1572872 | tf_op jit(solution)/shard_map/ppermute | solution.py:19
  5.0 7.9 %collective-permute-start.1 = (bf16[3072,256]{1,0:T(8,128)(2,1)}, bf16[3072,256]{1,0:T(8,128)(2,1)S(1)}, u32[]{:S(2)}, u32[]{:S(2)}) collective-permute-start(bf16[3072,256]{1,0:T(8,128)(2,1)} %own.3), channel_id=1, source_target_pairs={{0,1},{1,0},{2,3},{3,2},{4,5},{5,4},{6,7},{7,6},{8,9},{9,8},{10,11... | collective-permute-start | bytes 4718600 | tf_op jit(solution)/shard_map/ppermute | solution.py:19
  5.4 7.6 %collective-permute-start.2 = (bf16[256,1024]{1,0:T(8,128)(2,1)}, bf16[256,1024]{1,0:T(8,128)(2,1)S(1)}, u32[]{:S(2)}, u32[]{:S(2)}) collective-permute-start(bf16[256,1024]{1,0:T(8,128)(2,1)} %gb_own.3), channel_id=1, source_target_pairs={{0,1},{1,0},{2,3},{3,2},{4,5},{5,4},{6,7},{7,6},{8,9},{9,8},{10,11... | collective-permute-start | bytes 1572872 | tf_op jit(solution)/shard_map/ppermute | solution.py:19
  5.6 2.8 %copy-start = (bf16[3072,1024]{1,0:T(8,128)(2,1)S(1)}, bf16[3072,1024]{1,0:T(8,128)(2,1)}, u32[]{:S(2)}) copy-start(bf16[3072,1024]{1,0:T(8,128)(2,1)} %acts.1) | copy-start | bytes 18874372
  8.4 1.0 copy-start.3
  9.4 3.5 %copy-start.1 = (bf16[3072,256]{1,0:T(8,128)(2,1)S(1)}, bf16[3072,256]{1,0:T(8,128)(2,1)}, u32[]{:S(2)}) copy-start(bf16[3072,256]{1,0:T(8,128)(2,1)} %own.3) | copy-start | bytes 4718596
  9.4 3.5 %copy-start.2 = (bf16[256,1024]{1,0:T(8,128)(2,1)S(1)}, bf16[256,1024]{1,0:T(8,128)(2,1)}, u32[]{:S(2)}) copy-start(bf16[256,1024]{1,0:T(8,128)(2,1)} %gb_own.3) | copy-start | bytes 1572868
  12.1 7.6 %collective-permute-start.3 = (bf16[400,256]{1,0:T(8,128)(2,1)S(1)}, bf16[400,256]{1,0:T(8,128)(2,1)S(1)}, u32[]{:S(2)}, u32[]{:S(2)}) collective-permute-start(bf16[400,256]{1,0:T(8,128)(2,1)S(1)} %get-tuple-element.62), channel_id=1, source_target_pairs={{0,192},{32,224},{64,128},{96,160},{128,64},{160,96},{192,0},{224,... | collective-permute-start | bytes 614408 | tf_op jit(solution)/shard_map/ppermute | solution.py:24
  12.9 6.8 %collective-permute-start.4 = (bf16[400,256]{1,0:T(8,128)(2,1)S(1)}, bf16[400,256]{1,0:T(8,128)(2,1)S(1)}, u32[]{:S(2)}, u32[]{:S(2)}) collective-permute-start(bf16[400,256]{1,0:T(8,128)(2,1)S(1)} %get-tuple-element.63), channel_id=1, source_target_pairs={{0,64},{32,96},{64,0},{96,32},{128,192},{160,224},{192,128},{224,1... | collective-permute-start | bytes 614408 | tf_op jit(solution)/shard_map/ppermute | solution.py:24
  14.8 12.6 %collective-permute-start.5 = (bf16[400,512]{1,0:T(8,128)(2,1)S(1)}, bf16[400,512]{1,0:T(8,128)(2,1)S(1)}, u32[]{:S(2)}, u32[]{:S(2)}) collective-permute-start(bf16[400,512]{1,0:T(8,128)(2,1)S(1)} %get-tuple-element.56), channel_id=1, source_target_pairs={{0,6},{1,7},{2,4},{3,5},{4,2},{5,3},{6,0},{7,1},{8,14},{9,15},{10,... | collective-permute-start | bytes 1228808 | tf_op jit(solution)/shard_map/ppermute | solution.py:19
  17.6 9.8 %collective-permute-start.6 = (bf16[400,512]{1,0:T(8,128)(2,1)S(1)}, bf16[400,512]{1,0:T(8,128)(2,1)S(1)}, u32[]{:S(2)}, u32[]{:S(2)}) collective-permute-start(bf16[400,512]{1,0:T(8,128)(2,1)S(1)} %get-tuple-element.67), channel_id=1, source_target_pairs={{0,2},{1,3},{2,0},{3,1},{4,6},{5,7},{6,4},{7,5},{8,10},{9,11},{10,... | collective-permute-start | bytes 1228808 | tf_op jit(solution)/shard_map/ppermute | solution.py:19
  21.5 12.4 %collective-permute-start.8 = (bf16[400,512]{1,0:T(8,128)(2,1)S(1)}, bf16[400,512]{1,0:T(8,128)(2,1)S(1)}, u32[]{:S(2)}, u32[]{:S(2)}) collective-permute-start(bf16[400,512]{1,0:T(8,128)(2,1)S(1)} %get-tuple-element.72), channel_id=1, source_target_pairs={{0,192},{32,224},{64,128},{96,160},{128,64},{160,96},{192,0},{224,... | collective-permute-start | bytes 1228808 | tf_op jit(solution)/shard_map/ppermute | solution.py:24
  22.7 12.1 %collective-permute-start.7 = (bf16[400,512]{1,0:T(8,128)(2,1)S(1)}, bf16[400,512]{1,0:T(8,128)(2,1)S(1)}, u32[]{:S(2)}, u32[]{:S(2)}) collective-permute-start(bf16[400,512]{1,0:T(8,128)(2,1)S(1)} %get-tuple-element.64), channel_id=1, source_target_pairs={{0,64},{32,96},{64,0},{96,32},{128,192},{160,224},{192,128},{224,1... | collective-permute-start | bytes 1228808 | tf_op jit(solution)/shard_map/ppermute | solution.py:24
  29.3 14.1 %collective-permute-start.10 = (bf16[400,512]{1,0:T(8,128)(2,1)S(1)}, bf16[400,512]{1,0:T(8,128)(2,1)S(1)}, u32[]{:S(2)}, u32[]{:S(2)}) collective-permute-start(bf16[400,512]{1,0:T(8,128)(2,1)S(1)} %get-tuple-element.76), channel_id=1, source_target_pairs={{0,6},{1,7},{2,4},{3,5},{4,2},{5,3},{6,0},{7,1},{8,14},{9,15},{10,... | collective-permute-start | bytes 1228808 | tf_op jit(solution)/shard_map/ppermute | solution.py:19
  30.9 12.5 %collective-permute-start.9 = (bf16[400,512]{1,0:T(8,128)(2,1)S(1)}, bf16[400,512]{1,0:T(8,128)(2,1)S(1)}, u32[]{:S(2)}, u32[]{:S(2)}) collective-permute-start(bf16[400,512]{1,0:T(8,128)(2,1)S(1)} %get-tuple-element.68), channel_id=1, source_target_pairs={{0,2},{1,3},{2,0},{3,1},{4,6},{5,7},{6,4},{7,5},{8,10},{9,11},{10,... | collective-permute-start | bytes 1228808 | tf_op jit(solution)/shard_map/ppermute | solution.py:19
  32.7 15.6 %collective-permute-start.12 = (bf16[400,512]{1,0:T(8,128)(2,1)S(1)}, bf16[400,512]{1,0:T(8,128)(2,1)S(1)}, u32[]{:S(2)}, u32[]{:S(2)}) collective-permute-start(bf16[400,512]{1,0:T(8,128)(2,1)S(1)} %get-tuple-element.79), channel_id=1, source_target_pairs={{0,6},{1,7},{2,4},{3,5},{4,2},{5,3},{6,0},{7,1},{8,14},{9,15},{10,... | collective-permute-start | bytes 1228808 | tf_op jit(solution)/shard_map/ppermute | solution.py:19
  33.9 18.7 %collective-permute-start.11 = (bf16[400,512]{1,0:T(8,128)(2,1)S(1)}, bf16[400,512]{1,0:T(8,128)(2,1)S(1)}, u32[]{:S(2)}, u32[]{:S(2)}) collective-permute-start(bf16[400,512]{1,0:T(8,128)(2,1)S(1)} %get-tuple-element.70), channel_id=1, source_target_pairs={{0,2},{1,3},{2,0},{3,1},{4,6},{5,7},{6,4},{7,5},{8,10},{9,11},{10,... | collective-permute-start | bytes 1228808 | tf_op jit(solution)/shard_map/ppermute | solution.py:19
  36.3 26.6 %collective-permute-start.16 = (bf16[400,256]{1,0:T(8,128)(2,1)S(1)}, bf16[400,256]{1,0:T(8,128)(2,1)S(1)}, u32[]{:S(2)}, u32[]{:S(2)}) collective-permute-start(bf16[400,256]{1,0:T(8,128)(2,1)S(1)} %get-tuple-element.86), channel_id=1, source_target_pairs={{0,32},{32,0},{64,96},{96,64},{128,160},{160,128},{192,224},{224,1... | collective-permute-start | bytes 614408 | tf_op jit(solution)/shard_map/ppermute | solution.py:24
  45.0 13.4 %collective-permute-start.13 = (bf16[112,512]{1,0:T(8,128)(2,1)S(1)}, bf16[112,512]{1,0:T(8,128)(2,1)S(1)}, u32[]{:S(2)}, u32[]{:S(2)}) collective-permute-start(bf16[112,512]{1,0:T(8,128)(2,1)S(1)} %get-tuple-element.82), channel_id=1, source_target_pairs={{0,8},{1,9},{2,10},{3,11},{4,12},{5,13},{6,14},{7,15},{8,0},{9,1},... | collective-permute-start | bytes 344072 | tf_op jit(solution)/shard_map/ppermute | solution.py:19
  45.8 12.7 %collective-permute-start.14 = (bf16[112,512]{1,0:T(8,128)(2,1)S(1)}, bf16[112,512]{1,0:T(8,128)(2,1)S(1)}, u32[]{:S(2)}, u32[]{:S(2)}) collective-permute-start(bf16[112,512]{1,0:T(8,128)(2,1)S(1)} %get-tuple-element.83), channel_id=1, source_target_pairs={{0,16},{1,17},{2,18},{3,19},{4,20},{5,21},{6,22},{7,23},{8,24},{9,... | collective-permute-start | bytes 344072 | tf_op jit(solution)/shard_map/ppermute | solution.py:19
  48.2 12.2 %collective-permute-start.15 = (bf16[112,512]{1,0:T(8,128)(2,1)S(1)}, bf16[112,512]{1,0:T(8,128)(2,1)S(1)}, u32[]{:S(2)}, u32[]{:S(2)}) collective-permute-start(bf16[112,512]{1,0:T(8,128)(2,1)S(1)} %get-tuple-element.84), channel_id=1, source_target_pairs={{0,24},{1,25},{2,26},{3,27},{4,28},{5,29},{6,30},{7,31},{8,16},{9,... | collective-permute-start | bytes 344072 | tf_op jit(solution)/shard_map/ppermute | solution.py:19
  52.6 16.4 %collective-permute-start.17 = (bf16[400,256]{1,0:T(8,128)(2,1)S(1)}, bf16[400,256]{1,0:T(8,128)(2,1)S(1)}, u32[]{:S(2)}, u32[]{:S(2)}) collective-permute-start(bf16[400,256]{1,0:T(8,128)(2,1)S(1)} %get-tuple-element.87), channel_id=1, source_target_pairs={{0,32},{32,0},{64,96},{96,64},{128,160},{160,128},{192,224},{224,1... | collective-permute-start | bytes 614408 | tf_op jit(solution)/shard_map/ppermute | solution.py:24
  58.4 12.4 %collective-permute-start.18 = (bf16[112,512]{1,0:T(8,128)(2,1)S(1)}, bf16[112,512]{1,0:T(8,128)(2,1)S(1)}, u32[]{:S(2)}, u32[]{:S(2)}) collective-permute-start(bf16[112,512]{1,0:T(8,128)(2,1)S(1)} %get-tuple-element.89), channel_id=1, source_target_pairs={{0,8},{1,9},{2,10},{3,11},{4,12},{5,13},{6,14},{7,15},{8,0},{9,1},... | collective-permute-start | bytes 344072 | tf_op jit(solution)/shard_map/ppermute | solution.py:19
  58.5 21.2 %collective-permute-start.19 = (bf16[112,512]{1,0:T(8,128)(2,1)S(1)}, bf16[112,512]{1,0:T(8,128)(2,1)S(1)}, u32[]{:S(2)}, u32[]{:S(2)}) collective-permute-start(bf16[112,512]{1,0:T(8,128)(2,1)S(1)} %get-tuple-element.90), channel_id=1, source_target_pairs={{0,16},{1,17},{2,18},{3,19},{4,20},{5,21},{6,22},{7,23},{8,24},{9,... | collective-permute-start | bytes 344072 | tf_op jit(solution)/shard_map/ppermute | solution.py:19
  60.4 20.7 %collective-permute-start.20 = (bf16[112,512]{1,0:T(8,128)(2,1)S(1)}, bf16[112,512]{1,0:T(8,128)(2,1)S(1)}, u32[]{:S(2)}, u32[]{:S(2)}) collective-permute-start(bf16[112,512]{1,0:T(8,128)(2,1)S(1)} %get-tuple-element.91), channel_id=1, source_target_pairs={{0,24},{1,25},{2,26},{3,27},{4,28},{5,29},{6,30},{7,31},{8,16},{9,... | collective-permute-start | bytes 344072 | tf_op jit(solution)/shard_map/ppermute | solution.py:19
  62.9 21.1 %collective-permute-start.23 = (bf16[96,512]{1,0:T(8,128)(2,1)S(1)}, bf16[96,512]{1,0:T(8,128)(2,1)S(1)}, u32[]{:S(2)}, u32[]{:S(2)}) collective-permute-start(bf16[96,512]{1,0:T(8,128)(2,1)S(1)} %grad_round0.1.g0), channel_id=1, source_target_pairs={{0,24},{1,25},{2,26},{3,27},{4,28},{5,29},{6,30},{7,31},{8,16},{9,... | collective-permute-start | bytes 294920 | tf_op jit(solution)/shard_map/ppermute | solution.py:19
  69.9 20.5 %collective-permute-start.26 = (bf16[384,512]{1,0:T(8,128)(2,1)S(1)}, bf16[384,512]{1,0:T(8,128)(2,1)S(1)}, u32[]{:S(2)}, u32[]{:S(2)}) collective-permute-start(bf16[384,512]{1,0:T(8,128)(2,1)S(1)} %act_round.1.a0), channel_id=1, source_target_pairs={{0,192},{32,224},{64,128},{96,160},{128,64},{160,96},{192,0},{224,... | collective-permute-start | bytes 1179656 | tf_op jit(solution)/shard_map/ppermute | solution.py:24
  70.8 22.4 %collective-permute-start.25 = (bf16[384,512]{1,0:T(8,128)(2,1)S(1)}, bf16[384,512]{1,0:T(8,128)(2,1)S(1)}, u32[]{:S(2)}, u32[]{:S(2)}) collective-permute-start(bf16[384,512]{1,0:T(8,128)(2,1)S(1)} %act_round.1.a0), channel_id=1, source_target_pairs={{0,128},{32,160},{64,192},{96,224},{128,0},{160,32},{192,64},{224,... | collective-permute-start | bytes 1179656 | tf_op jit(solution)/shard_map/ppermute | solution.py:24
  79.8 13.4 %collective-permute-start.24 = (bf16[384,512]{1,0:T(8,128)(2,1)S(1)}, bf16[384,512]{1,0:T(8,128)(2,1)S(1)}, u32[]{:S(2)}, u32[]{:S(2)}) collective-permute-start(bf16[384,512]{1,0:T(8,128)(2,1)S(1)} %act_round.1.a0), channel_id=1, source_target_pairs={{0,64},{32,96},{64,0},{96,32},{128,192},{160,224},{192,128},{224,1... | collective-permute-start | bytes 1179656 | tf_op jit(solution)/shard_map/ppermute | solution.py:24
  81.1 5.4 %collective-permute-start.22 = (bf16[96,512]{1,0:T(8,128)(2,1)S(1)}, bf16[96,512]{1,0:T(8,128)(2,1)S(1)}, u32[]{:S(2)}, u32[]{:S(2)}) collective-permute-start(bf16[96,512]{1,0:T(8,128)(2,1)S(1)} %grad_round0.1.g0), channel_id=1, source_target_pairs={{0,16},{1,17},{2,18},{3,19},{4,20},{5,21},{6,22},{7,23},{8,24},{9,... | collective-permute-start | bytes 294920 | tf_op jit(solution)/shard_map/ppermute | solution.py:19
  84.0 3.8 %collective-permute-start.21 = (bf16[96,512]{1,0:T(8,128)(2,1)S(1)}, bf16[96,512]{1,0:T(8,128)(2,1)S(1)}, u32[]{:S(2)}, u32[]{:S(2)}) collective-permute-start(bf16[96,512]{1,0:T(8,128)(2,1)S(1)} %grad_round0.1.g0), channel_id=1, source_target_pairs={{0,8},{1,9},{2,10},{3,11},{4,12},{5,13},{6,14},{7,15},{8,0},{9,1},... | collective-permute-start | bytes 294920 | tf_op jit(solution)/shard_map/ppermute | solution.py:19
  88.4 11.8 %collective-permute-start.28 = (bf16[2,384,256]{2,1,0:T(8,128)(2,1)S(1)}, bf16[2,384,256]{2,1,0:T(8,128)(2,1)S(1)}, u32[]{:S(2)}, u32[]{:S(2)}) collective-permute-start(bf16[2,384,256]{2,1,0:T(8,128)(2,1)S(1)} %grad_join0.1.g), channel_id=1, source_target_pairs={{0,6},{1,7},{2,4},{3,5},{4,2},{5,3},{6,0},{7,1},{8,14},{9,15},{10,... | collective-permute-start | bytes 1179656 | tf_op jit(solution)/shard_map/ppermute | solution.py:19
  90.1 11.5 %collective-permute-start.27 = (bf16[2,384,256]{2,1,0:T(8,128)(2,1)S(1)}, bf16[2,384,256]{2,1,0:T(8,128)(2,1)S(1)}, u32[]{:S(2)}, u32[]{:S(2)}) collective-permute-start(bf16[2,384,256]{2,1,0:T(8,128)(2,1)S(1)} %grad_join0.1.g), channel_id=1, source_target_pairs={{0,2},{1,3},{2,0},{3,1},{4,6},{5,7},{6,4},{7,5},{8,10},{9,11},{10,... | collective-permute-start | bytes 1179656 | tf_op jit(solution)/shard_map/ppermute | solution.py:19
  90.5 5.3 %collective-permute-start.34 = (bf16[96,512]{1,0:T(8,128)(2,1)S(1)}, bf16[96,512]{1,0:T(8,128)(2,1)S(1)}, u32[]{:S(2)}, u32[]{:S(2)}) collective-permute-start(bf16[96,512]{1,0:T(8,128)(2,1)S(1)} %grad_round1.1.g0), channel_id=1, source_target_pairs={{0,24},{1,25},{2,26},{3,27},{4,28},{5,29},{6,30},{7,31},{8,16},{9,... | collective-permute-start | bytes 294920 | tf_op jit(solution)/shard_map/ppermute | solution.py:19
  93.2 4.6 %collective-permute-start.33 = (bf16[96,512]{1,0:T(8,128)(2,1)S(1)}, bf16[96,512]{1,0:T(8,128)(2,1)S(1)}, u32[]{:S(2)}, u32[]{:S(2)}) collective-permute-start(bf16[96,512]{1,0:T(8,128)(2,1)S(1)} %grad_round1.1.g0), channel_id=1, source_target_pairs={{0,16},{1,17},{2,18},{3,19},{4,20},{5,21},{6,22},{7,23},{8,24},{9,... | collective-permute-start | bytes 294920 | tf_op jit(solution)/shard_map/ppermute | solution.py:19
  93.2 4.6 %collective-permute-start.32 = (bf16[96,512]{1,0:T(8,128)(2,1)S(1)}, bf16[96,512]{1,0:T(8,128)(2,1)S(1)}, u32[]{:S(2)}, u32[]{:S(2)}) collective-permute-start(bf16[96,512]{1,0:T(8,128)(2,1)S(1)} %grad_round1.1.g0), channel_id=1, source_target_pairs={{0,8},{1,9},{2,10},{3,11},{4,12},{5,13},{6,14},{7,15},{8,0},{9,1},... | collective-permute-start | bytes 294920 | tf_op jit(solution)/shard_map/ppermute | solution.py:19
  98.4 10.1 %collective-permute-start.36 = (bf16[2,384,256]{2,1,0:T(8,128)(2,1)S(1)}, bf16[2,384,256]{2,1,0:T(8,128)(2,1)S(1)}, u32[]{:S(2)}, u32[]{:S(2)}) collective-permute-start(bf16[2,384,256]{2,1,0:T(8,128)(2,1)S(1)} %grad_join1.1.g), channel_id=1, source_target_pairs={{0,6},{1,7},{2,4},{3,5},{4,2},{5,3},{6,0},{7,1},{8,14},{9,15},{10,... | collective-permute-start | bytes 1179656 | tf_op jit(solution)/shard_map/ppermute | solution.py:19
  100.0 10.1 %collective-permute-start.35 = (bf16[2,384,256]{2,1,0:T(8,128)(2,1)S(1)}, bf16[2,384,256]{2,1,0:T(8,128)(2,1)S(1)}, u32[]{:S(2)}, u32[]{:S(2)}) collective-permute-start(bf16[2,384,256]{2,1,0:T(8,128)(2,1)S(1)} %grad_join1.1.g), channel_id=1, source_target_pairs={{0,2},{1,3},{2,0},{3,1},{4,6},{5,7},{6,4},{7,5},{8,10},{9,11},{10,... | collective-permute-start | bytes 1179656 | tf_op jit(solution)/shard_map/ppermute | solution.py:19
  100.2 13.0 %collective-permute-start.30 = (bf16[384,256]{1,0:T(8,128)(2,1)S(1)}, bf16[384,256]{1,0:T(8,128)(2,1)S(1)}, u32[]{:S(2)}, u32[]{:S(2)}) collective-permute-start(bf16[384,256]{1,0:T(8,128)(2,1)S(1)} %slice_bitcast_fusion.2), channel_id=1, source_target_pairs={{0,2},{1,3},{2,0},{3,1},{4,6},{5,7},{6,4},{7,5},{8,10},{9,11},{10,... | collective-permute-start | bytes 589832 | tf_op jit(solution)/shard_map/ppermute | solution.py:19
  101.6 11.5 %collective-permute-start.29 = (bf16[384,256]{1,0:T(8,128)(2,1)S(1)}, bf16[384,256]{1,0:T(8,128)(2,1)S(1)}, u32[]{:S(2)}, u32[]{:S(2)}) collective-permute-start(bf16[384,256]{1,0:T(8,128)(2,1)S(1)} %slice_bitcast_fusion.3), channel_id=1, source_target_pairs={{0,6},{1,7},{2,4},{3,5},{4,2},{5,3},{6,0},{7,1},{8,14},{9,15},{10,... | collective-permute-start | bytes 589832 | tf_op jit(solution)/shard_map/ppermute | solution.py:19
  108.5 14.5 %collective-permute-start.38 = (bf16[384,256]{1,0:T(8,128)(2,1)S(1)}, bf16[384,256]{1,0:T(8,128)(2,1)S(1)}, u32[]{:S(2)}, u32[]{:S(2)}) collective-permute-start(bf16[384,256]{1,0:T(8,128)(2,1)S(1)} %slice_bitcast_fusion), channel_id=1, source_target_pairs={{0,2},{1,3},{2,0},{3,1},{4,6},{5,7},{6,4},{7,5},{8,10},{9,11},{10,... | collective-permute-start | bytes 589832 | tf_op jit(solution)/shard_map/ppermute | solution.py:19
  110.2 12.9 %collective-permute-start.37 = (bf16[384,256]{1,0:T(8,128)(2,1)S(1)}, bf16[384,256]{1,0:T(8,128)(2,1)S(1)}, u32[]{:S(2)}, u32[]{:S(2)}) collective-permute-start(bf16[384,256]{1,0:T(8,128)(2,1)S(1)} %slice_bitcast_fusion.1), channel_id=1, source_target_pairs={{0,6},{1,7},{2,4},{3,5},{4,2},{5,3},{6,0},{7,1},{8,14},{9,15},{10,... | collective-permute-start | bytes 589832 | tf_op jit(solution)/shard_map/ppermute | solution.py:19
  114.7 13.2 %collective-permute-start.31 = (f32[512,256]{1,0:T(8,128)S(1)}, f32[512,256]{1,0:T(8,128)S(1)}, u32[]{:S(2)}, u32[]{:S(2)}) collective-permute-start(f32[512,256]{1,0:T(8,128)S(1)} %get-tuple-element.95), channel_id=1, source_target_pairs={{0,1},{1,0},{2,3},{3,2},{4,5},{5,4},{6,7},{7,6},{8,9},{9,8},{10,11... | collective-permute-start | bytes 1572872 | tf_op jit(solution)/shard_map/ppermute | solution.py:19
  124.7 4.8 %collective-permute-start.39 = (f32[512,256]{1,0:T(8,128)S(1)}, f32[512,256]{1,0:T(8,128)S(1)}, u32[]{:S(2)}, u32[]{:S(2)}) collective-permute-start(f32[512,256]{1,0:T(8,128)S(1)} %get-tuple-element.98), channel_id=1, source_target_pairs={{0,1},{1,0},{2,3},{3,2},{4,5},{5,4},{6,7},{7,6},{8,9},{9,8},{10,11... | collective-permute-start | bytes 1572872 | tf_op jit(solution)/shard_map/ppermute | solution.py:19

commit v3 on v2

--- a/solution.py
+++ b/solution.py
@@ -308,7 +308,7 @@
             f"grad_round{pair}",
         )
         token = g_own
-        g_all.append([g_own, *[col_swap(g_own, z=k) for k in (1, 2, 3)]])
+        g_all.append([g_own, *[col_swap(g_own, z=k) for k in (3, 2, 1)][::-1]])
         if pair == 0:
             (a_own,) = call(
                 act_round, after(place, token), [(a_shape, BF16)], (a_total, *a_got2), None, "act_round"

time: 131 us -> 131 us (level)
  no operation moved by 1% of the time
where the time goes in v3:
time: 131 us
  starting transfers between devices  66.9 us (51%)
  waiting for transfers between devices  34.2 us (26%)
  Pallas kernels  25.8 us (20%)
  local copies, waits for them, and re-layouts  3.89 us (3%)
    ppermute x31, starting transfers between devices, col_swap(): return lax.ppermute(a, 'col', perm)  48.6 us
    ppermute x31, waiting for transfers between devices, col_swap(): return lax.ppermute(a, 'col', perm)  29.7 us
    pallas_call x18, Pallas kernels, call(): pl.pallas_call(body, out_shape=[jax.ShapeDtypeStruct(s, d) for s, d in ou...  25.8 us
    ppermute x9, starting transfers between devices, row_swap(): return lax.ppermute(a, 'row', perm)  18.2 us
    ppermute x9, waiting for transfers between devices, row_swap(): return lax.ppermute(a, 'row', perm)  4.46 us
    unnamed x8, local copies, waits for them, and re-layouts  3.83 us
  transfers between devices with their start and end apart: 40, of which 14 were waited for; matrix products, arithmetic and copies ran while one was open for 0% of the time, Pallas kernels for 18%

profile of v3, /device:TPU:1, one launch (start us, length us, event | category | flops | bytes accessed | tf_op | source)
XLA Modules:
  0.0 131.1 jit_solution(17774073367878188326)
XLA Ops:
  0.0 3.2 %collective-permute-start = (bf16[1024,256]{1,0:T(8,128)(2,1)}, bf16[1024,256]{1,0:T(8,128)(2,1)S(1)}, u32[]{:S(2)}, u32[]{:S(2)}) collective-permute-start(bf16[1024,256]{1,0:T(8,128)(2,1)} %ab_own.1), channel_id=1, source_target_pairs={{0,1},{1,0},{2,3},{3,2},{4,5},{5,4},{6,7},{7,6},{8,9},{9,8},{10,11... | collective-permute-start | bytes 1572872 | tf_op jit(solution)/shard_map/ppermute | solution.py:19
  3.2 1.7 %collective-permute-done.ab_got = bf16[1024,256]{1,0:T(8,128)(2,1)S(1)} collective-permute-done((bf16[1024,256]{1,0:T(8,128)(2,1)}, bf16[1024,256]{1,0:T(8,128)(2,1)S(1)}, u32[]{:S(2)}, u32[]{:S(2)}) %collective-permute-start) | collective-permute-done | bytes 524320 | tf_op jit(solution)/shard_map/ppermute | solution.py:19
  5.0 0.4 collective-permute-start.1
  5.6 2.8 %copy-done = bf16[3072,1024]{1,0:T(8,128)(2,1)S(1)} copy-done((bf16[3072,1024]{1,0:T(8,128)(2,1)S(1)}, bf16[3072,1024]{1,0:T(8,128)(2,1)}, u32[]{:S(2)}) %copy-start) | copy-done | bytes 6291480
  8.4 1.0 copy-done.3
  9.4 2.7 %act_first.1 = (bf16[400,256]{1,0:T(8,128)(2,1)S(1)}, bf16[400,256]{1,0:T(8,128)(2,1)S(1)}, f32[384,512]{1,0:T(8,128)S(1)}, f32[384,512]{1,0:T(8,128)S(1)}, f32[384,512]{1,0:T(8,128)S(1)}) custom-call(s32[4]{0:T(128)S(1)} %pad_add_fusion.place, bf16[3072,1024]{1,0:T(8,128)(2,1)S(1)} %copy-done, bf16[1024,256]{1,0:T(8,128)(2,1)S(1)} %copy-done.3, ...), custom_call_target="tpu_custom_call" | custom-call | flops 1610612736 | bytes 10108928 | tf_op jit(solution)/shard_map/act_first/pallas_call | solution.py:68
  12.1 0.8 collective-permute-start.3
  12.9 1.9 %grad_first.1 = (bf16[400,512]{1,0:T(8,128)(2,1)S(1)}, bf16[400,512]{1,0:T(8,128)(2,1)S(1)}) custom-call(s32[4]{0:T(128)S(1)} %pad_add_fusion.place, bf16[3072,256]{1,0:T(8,128)(2,1)S(1)} %copy-done.1, bf16[3072,256]{1,0:T(8,128)(2,1)S(1)} %collective-permute-done.1.got, bf16[256,1024]{1,0:T(8,128)(2,1)S(1)} %copy-done.2, ...), custom_call_target="tpu_custom_call" | custom-call | flops 402653184 | bytes 5013504 | tf_op jit(solution)/shard_map/grad_first/pallas_call | solution.py:68
  14.8 2.8 %collective-permute-start.5 = (bf16[400,512]{1,0:T(8,128)(2,1)S(1)}, bf16[400,512]{1,0:T(8,128)(2,1)S(1)}, u32[]{:S(2)}, u32[]{:S(2)}) collective-permute-start(bf16[400,512]{1,0:T(8,128)(2,1)S(1)} %get-tuple-element.56), channel_id=1, source_target_pairs={{0,6},{1,7},{2,4},{3,5},{4,2},{5,3},{6,0},{7,1},{8,14},{9,15},{10,... | collective-permute-start | bytes 1228808 | tf_op jit(solution)/shard_map/ppermute | solution.py:19
  17.7 1.9 %grad_rest.1 = (f32[384,1024]{1,0:T(8,128)S(1)}, f32[384,1024]{1,0:T(8,128)S(1)}, f32[384,1024]{1,0:T(8,128)S(1)}) custom-call(s32[4]{0:T(128)S(1)} %pad_add_fusion.place, bf16[3072,256]{1,0:T(8,128)(2,1)S(1)} %copy-done.1, bf16[3072,256]{1,0:T(8,128)(2,1)S(1)} %collective-permute-done.1.got, bf16[256,1024]{1,0:T(8,128)(2,1)S(1)} %copy-done.2, ...), custom_call_target="tpu_custom_call" | custom-call | flops 1207959552 | bytes 8912896 | tf_op jit(solution)/shard_map/grad_rest/pallas_call | solution.py:68
  19.7 1.8 %act_mid.1 = (bf16[400,512]{1,0:T(8,128)(2,1)S(1)}, bf16[400,512]{1,0:T(8,128)(2,1)S(1)}) custom-call(s32[4]{0:T(128)S(1)} %pad_add_fusion.place, f32[384,512]{1,0:T(8,128)S(1)} %get-tuple-element.60.keep1, f32[384,512]{1,0:T(8,128)S(1)} %get-tuple-element.61.keep3, bf16[400,256]{1,0:T(8,128)(2,1)S(1)} %collective-permute-done.3.got_a, ...), custom_call_target="tpu_custom_call" | custom-call | bytes 2801664 | tf_op jit(solution)/shard_map/act_mid/pallas_call | solution.py:68
  21.5 1.2 collective-permute-start.8
  23.1 4.4 %collective-permute-done.6.got_b = bf16[400,512]{1,0:T(8,128)(2,1)S(1)} collective-permute-done((bf16[400,512]{1,0:T(8,128)(2,1)S(1)}, bf16[400,512]{1,0:T(8,128)(2,1)S(1)}, u32[]{:S(2)}, u32[]{:S(2)}) %collective-permute-start.6) | collective-permute-done | bytes 409632 | tf_op jit(solution)/shard_map/ppermute | solution.py:19
  27.5 1.8 %grad_second0.1 = (bf16[400,512]{1,0:T(8,128)(2,1)S(1)}, bf16[400,512]{1,0:T(8,128)(2,1)S(1)}) custom-call(s32[4]{0:T(128)S(1)} %pad_add_fusion.place, f32[384,1024]{1,0:T(8,128)S(1)} %get-tuple-element.58.p1, f32[384,1024]{1,0:T(8,128)S(1)} %get-tuple-element.66.p3, bf16[400,512]{1,0:T(8,128)(2,1)S(1)} %collective-permute-done.5.got_a, ...), custom_call_target="tpu_custom_call" | custom-call | bytes 4784128 | tf_op jit(solution)/shard_map/grad_second0/pallas_call | solution.py:68
  29.3 1.6 %collective-permute-start.10 = (bf16[400,512]{1,0:T(8,128)(2,1)S(1)}, bf16[400,512]{1,0:T(8,128)(2,1)S(1)}, u32[]{:S(2)}, u32[]{:S(2)}) collective-permute-start(bf16[400,512]{1,0:T(8,128)(2,1)S(1)} %get-tuple-element.76), channel_id=1, source_target_pairs={{0,6},{1,7},{2,4},{3,5},{4,2},{5,3},{6,0},{7,1},{8,14},{9,15},{10,... | collective-permute-start | bytes 1228808 | tf_op jit(solution)/shard_map/ppermute | solution.py:19
  30.9 1.8 %grad_second1.1 = (bf16[400,512]{1,0:T(8,128)(2,1)S(1)}, bf16[400,512]{1,0:T(8,128)(2,1)S(1)}) custom-call(s32[4]{0:T(128)S(1)} %pad_add_fusion.place, f32[384,1024]{1,0:T(8,128)S(1)} %get-tuple-element.58.p1, f32[384,1024]{1,0:T(8,128)S(1)} %get-tuple-element.66.p3, bf16[400,512]{1,0:T(8,128)(2,1)S(1)} %collective-permute-done.5.got_a, ...), custom_call_target="tpu_custom_call" | custom-call | bytes 4784128 | tf_op jit(solution)/shard_map/grad_second1/pallas_call | solution.py:68
  32.7 1.3 collective-permute-start.12
  33.9 0.9 collective-permute-start.11
  34.8 1.5 %act_second.1 = (f32[384,512]{1,0:T(8,128)S(1)}, bf16[400,256]{1,0:T(8,128)(2,1)S(1)}, bf16[400,256]{1,0:T(8,128)(2,1)S(1)}) custom-call(s32[4]{0:T(128)S(1)} %pad_add_fusion.place, f32[384,512]{1,0:T(8,128)S(1)} %get-tuple-element.52.keep, bf16[400,512]{1,0:T(8,128)(2,1)S(1)} %collective-permute-done.7.got_p, bf16[400,512]{1,0:T(8,128)(2,1)S(1)} %collective-permute-done.8.got_q), custom_call_target="tpu_custom_call" | custom-call | bytes 2801664 | tf_op jit(solution)/shard_map/act_second/pallas_call | solution.py:68
  36.3 7.0 %collective-permute-start.16 = (bf16[400,256]{1,0:T(8,128)(2,1)S(1)}, bf16[400,256]{1,0:T(8,128)(2,1)S(1)}, u32[]{:S(2)}, u32[]{:S(2)}) collective-permute-start(bf16[400,256]{1,0:T(8,128)(2,1)S(1)} %get-tuple-element.86), channel_id=1, source_target_pairs={{0,32},{32,0},{64,96},{96,64},{128,160},{160,128},{192,224},{224,1... | collective-permute-start | bytes 614408 | tf_op jit(solution)/shard_map/ppermute | solution.py:24
  43.3 1.6 %grad_z0.1 = (bf16[112,512]{1,0:T(8,128)(2,1)S(1)}, bf16[112,512]{1,0:T(8,128)(2,1)S(1)}, bf16[112,512]{1,0:T(8,128)(2,1)S(1)}, f32[96,512]{1,0:T(8,128)S(1)}) custom-call(s32[4]{0:T(128)S(1)} %pad_add_fusion.place, f32[384,1024]{1,0:T(8,128)S(1)} %get-tuple-element.75.p0, bf16[400,512]{1,0:T(8,128)(2,1)S(1)} %collective-permute-done.9.got_p, ...), custom_call_target="tpu_custom_call" | custom-call | bytes 2932736 | tf_op jit(solution)/shard_map/grad_z0/pallas_call | solution.py:68
  45.0 0.8 collective-permute-start.13
  45.8 1.2 collective-permute-start.14
  47.0 1.2 collective-permute-done.12.got_q
  48.2 4.3 %collective-permute-start.15 = (bf16[112,512]{1,0:T(8,128)(2,1)S(1)}, bf16[112,512]{1,0:T(8,128)(2,1)S(1)}, u32[]{:S(2)}, u32[]{:S(2)}) collective-permute-start(bf16[112,512]{1,0:T(8,128)(2,1)S(1)} %get-tuple-element.84), channel_id=1, source_target_pairs={{0,24},{1,25},{2,26},{3,27},{4,28},{5,29},{6,30},{7,31},{8,16},{9,... | collective-permute-start | bytes 344072 | tf_op jit(solution)/shard_map/ppermute | solution.py:19
  52.6 4.2 %collective-permute-start.17 = (bf16[400,256]{1,0:T(8,128)(2,1)S(1)}, bf16[400,256]{1,0:T(8,128)(2,1)S(1)}, u32[]{:S(2)}, u32[]{:S(2)}) collective-permute-start(bf16[400,256]{1,0:T(8,128)(2,1)S(1)} %get-tuple-element.87), channel_id=1, source_target_pairs={{0,32},{32,0},{64,96},{96,64},{128,160},{160,128},{192,224},{224,1... | collective-permute-start | bytes 614408 | tf_op jit(solution)/shard_map/ppermute | solution.py:24
  56.8 1.6 %grad_z1.1 = (bf16[112,512]{1,0:T(8,128)(2,1)S(1)}, bf16[112,512]{1,0:T(8,128)(2,1)S(1)}, bf16[112,512]{1,0:T(8,128)(2,1)S(1)}, f32[96,512]{1,0:T(8,128)S(1)}) custom-call(s32[4]{0:T(128)S(1)} %pad_add_fusion.place, f32[384,1024]{1,0:T(8,128)S(1)} %get-tuple-element.75.p0, bf16[400,512]{1,0:T(8,128)(2,1)S(1)} %collective-permute-done.11.got_p, ...), custom_call_target="tpu_custom_call" | custom-call | bytes 2932736 | tf_op jit(solution)/shard_map/grad_z1/pallas_call | solution.py:68
  58.5 1.9 %collective-permute-start.19 = (bf16[112,512]{1,0:T(8,128)(2,1)S(1)}, bf16[112,512]{1,0:T(8,128)(2,1)S(1)}, u32[]{:S(2)}, u32[]{:S(2)}) collective-permute-start(bf16[112,512]{1,0:T(8,128)(2,1)S(1)} %get-tuple-element.90), channel_id=1, source_target_pairs={{0,16},{1,17},{2,18},{3,19},{4,20},{5,21},{6,22},{7,23},{8,24},{9,... | collective-permute-start | bytes 344072 | tf_op jit(solution)/shard_map/ppermute | solution.py:19
  60.4 1.6 %collective-permute-start.20 = (bf16[112,512]{1,0:T(8,128)(2,1)S(1)}, bf16[112,512]{1,0:T(8,128)(2,1)S(1)}, u32[]{:S(2)}, u32[]{:S(2)}) collective-permute-start(bf16[112,512]{1,0:T(8,128)(2,1)S(1)} %get-tuple-element.91), channel_id=1, source_target_pairs={{0,24},{1,25},{2,26},{3,27},{4,28},{5,29},{6,30},{7,31},{8,16},{9,... | collective-permute-start | bytes 344072 | tf_op jit(solution)/shard_map/ppermute | solution.py:19
  62.1 0.8 grad_round0.1.g0
  62.9 1.7 %collective-permute-start.23 = (bf16[96,512]{1,0:T(8,128)(2,1)S(1)}, bf16[96,512]{1,0:T(8,128)(2,1)S(1)}, u32[]{:S(2)}, u32[]{:S(2)}) collective-permute-start(bf16[96,512]{1,0:T(8,128)(2,1)S(1)} %grad_round0.1.g0), channel_id=1, source_target_pairs={{0,24},{1,25},{2,26},{3,27},{4,28},{5,29},{6,30},{7,31},{8,16},{9,... | collective-permute-start | bytes 294920 | tf_op jit(solution)/shard_map/ppermute | solution.py:19
  64.6 4.4 %collective-permute-done.17.refs_1_ = bf16[400,256]{1,0:T(8,128)(2,1)S(1)} collective-permute-done((bf16[400,256]{1,0:T(8,128)(2,1)S(1)}, bf16[400,256]{1,0:T(8,128)(2,1)S(1)}, u32[]{:S(2)}, u32[]{:S(2)}) %collective-permute-start.17) | collective-permute-done | bytes 204832 | tf_op jit(solution)/shard_map/ppermute | solution.py:24
  69.0 1.0 act_round.1.a0
  69.9 0.8 collective-permute-start.26
  70.8 2.4 %collective-permute-start.25 = (bf16[384,512]{1,0:T(8,128)(2,1)S(1)}, bf16[384,512]{1,0:T(8,128)(2,1)S(1)}, u32[]{:S(2)}, u32[]{:S(2)}) collective-permute-start(bf16[384,512]{1,0:T(8,128)(2,1)S(1)} %act_round.1.a0), channel_id=1, source_target_pairs={{0,128},{32,160},{64,192},{96,224},{128,0},{160,32},{192,64},{224,... | collective-permute-start | bytes 1179656 | tf_op jit(solution)/shard_map/ppermute | solution.py:24
  73.2 6.6 %collective-permute-done.19.got2 = bf16[112,512]{1,0:T(8,128)(2,1)S(1)} collective-permute-done((bf16[112,512]{1,0:T(8,128)(2,1)S(1)}, bf16[112,512]{1,0:T(8,128)(2,1)S(1)}, u32[]{:S(2)}, u32[]{:S(2)}) %collective-permute-start.19) | collective-permute-done | bytes 114720 | tf_op jit(solution)/shard_map/ppermute | solution.py:19
  79.8 1.3 %collective-permute-start.24 = (bf16[384,512]{1,0:T(8,128)(2,1)S(1)}, bf16[384,512]{1,0:T(8,128)(2,1)S(1)}, u32[]{:S(2)}, u32[]{:S(2)}) collective-permute-start(bf16[384,512]{1,0:T(8,128)(2,1)S(1)} %act_round.1.a0), channel_id=1, source_target_pairs={{0,64},{32,96},{64,0},{96,32},{128,192},{160,224},{192,128},{224,1... | collective-permute-start | bytes 1179656 | tf_op jit(solution)/shard_map/ppermute | solution.py:24
  81.1 2.9 %collective-permute-start.22 = (bf16[96,512]{1,0:T(8,128)(2,1)S(1)}, bf16[96,512]{1,0:T(8,128)(2,1)S(1)}, u32[]{:S(2)}, u32[]{:S(2)}) collective-permute-start(bf16[96,512]{1,0:T(8,128)(2,1)S(1)} %grad_round0.1.g0), channel_id=1, source_target_pairs={{0,16},{1,17},{2,18},{3,19},{4,20},{5,21},{6,22},{7,23},{8,24},{9,... | collective-permute-start | bytes 294920 | tf_op jit(solution)/shard_map/ppermute | solution.py:19
  84.0 0.9 collective-permute-start.21
  84.9 0.8 grad_round1.1.g0
  85.7 0.8 collective-permute-done.22.g2
  86.5 1.3 collective-permute-done.21.g1
  87.8 0.6 grad_join0.1.g
  88.4 1.7 %collective-permute-start.28 = (bf16[2,384,256]{2,1,0:T(8,128)(2,1)S(1)}, bf16[2,384,256]{2,1,0:T(8,128)(2,1)S(1)}, u32[]{:S(2)}, u32[]{:S(2)}) collective-permute-start(bf16[2,384,256]{2,1,0:T(8,128)(2,1)S(1)} %grad_join0.1.g), channel_id=1, source_target_pairs={{0,6},{1,7},{2,4},{3,5},{4,2},{5,3},{6,0},{7,1},{8,14},{9,15},{10,... | collective-permute-start | bytes 1179656 | tf_op jit(solution)/shard_map/ppermute | solution.py:19
  90.1 0.4 collective-permute-start.27
  90.5 2.8 %collective-permute-start.34 = (bf16[96,512]{1,0:T(8,128)(2,1)S(1)}, bf16[96,512]{1,0:T(8,128)(2,1)S(1)}, u32[]{:S(2)}, u32[]{:S(2)}) collective-permute-start(bf16[96,512]{1,0:T(8,128)(2,1)S(1)} %grad_round1.1.g0), channel_id=1, source_target_pairs={{0,24},{1,25},{2,26},{3,27},{4,28},{5,29},{6,30},{7,31},{8,16},{9,... | collective-permute-start | bytes 294920 | tf_op jit(solution)/shard_map/ppermute | solution.py:19
  93.2 0.8 collective-permute-start.32
  94.0 0.6 act_join.1.acts
  94.7 1.1 collective-permute-done.34.g3
  95.8 2.1 %collective-permute-done.33.g2 = bf16[96,512]{1,0:T(8,128)(2,1)S(1)} collective-permute-done((bf16[96,512]{1,0:T(8,128)(2,1)S(1)}, bf16[96,512]{1,0:T(8,128)(2,1)S(1)}, u32[]{:S(2)}, u32[]{:S(2)}) %collective-permute-start.33) | collective-permute-done | bytes 98336 | tf_op jit(solution)/shard_map/ppermute | solution.py:19
  97.9 0.6 grad_join1.1.g
  98.4 1.6 %collective-permute-start.36 = (bf16[2,384,256]{2,1,0:T(8,128)(2,1)S(1)}, bf16[2,384,256]{2,1,0:T(8,128)(2,1)S(1)}, u32[]{:S(2)}, u32[]{:S(2)}) collective-permute-start(bf16[2,384,256]{2,1,0:T(8,128)(2,1)S(1)} %grad_join1.1.g), channel_id=1, source_target_pairs={{0,6},{1,7},{2,4},{3,5},{4,2},{5,3},{6,0},{7,1},{8,14},{9,15},{10,... | collective-permute-start | bytes 1179656 | tf_op jit(solution)/shard_map/ppermute | solution.py:19
  100.2 1.5 %collective-permute-start.30 = (bf16[384,256]{1,0:T(8,128)(2,1)S(1)}, bf16[384,256]{1,0:T(8,128)(2,1)S(1)}, u32[]{:S(2)}, u32[]{:S(2)}) collective-permute-start(bf16[384,256]{1,0:T(8,128)(2,1)S(1)} %slice_bitcast_fusion.2), channel_id=1, source_target_pairs={{0,2},{1,3},{2,0},{3,1},{4,6},{5,7},{6,4},{7,5},{8,10},{9,11},{10,... | collective-permute-start | bytes 589832 | tf_op jit(solution)/shard_map/ppermute | solution.py:19
  101.6 1.3 collective-permute-start.29
  102.9 5.6 %collective-permute-done.36.g_q = bf16[2,384,256]{2,1,0:T(8,128)(2,1)S(1)} collective-permute-done((bf16[2,384,256]{2,1,0:T(8,128)(2,1)S(1)}, bf16[2,384,256]{2,1,0:T(8,128)(2,1)S(1)}, u32[]{:S(2)}, u32[]{:S(2)}) %collective-permute-start.36) | collective-permute-done | bytes 393248 | tf_op jit(solution)/shard_map/ppermute | solution.py:19
  108.6 1.5 %collective-permute-done.35.g_p = bf16[2,384,256]{2,1,0:T(8,128)(2,1)S(1)} collective-permute-done((bf16[2,384,256]{2,1,0:T(8,128)(2,1)S(1)}, bf16[2,384,256]{2,1,0:T(8,128)(2,1)S(1)}, u32[]{:S(2)}, u32[]{:S(2)}) %collective-permute-start.35) | collective-permute-done | bytes 393248 | tf_op jit(solution)/shard_map/ppermute | solution.py:19
  110.2 1.2 collective-permute-start.37
  111.3 1.8 %collective-permute-done.30.far_b = bf16[384,256]{1,0:T(8,128)(2,1)S(1)} collective-permute-done((bf16[384,256]{1,0:T(8,128)(2,1)S(1)}, bf16[384,256]{1,0:T(8,128)(2,1)S(1)}, u32[]{:S(2)}, u32[]{:S(2)}) %collective-permute-start.30) | collective-permute-done | bytes 196640 | tf_op jit(solution)/shard_map/ppermute | solution.py:19
  113.1 1.6 %square0.1 = (f32[512,256]{1,0:T(8,128)S(1)}, f32[512,256]{1,0:T(8,128)S(1)}) custom-call(s32[4]{0:T(128)S(1)} %pad_add_fusion.place, bf16[3,512,512]{2,1,0:T(8,128)(2,1)S(1)} %act_join.1.acts, bf16[2,384,256]{2,1,0:T(8,128)(2,1)S(1)} %grad_join0.1.g, bf16[2,384,256]{2,1,0:T(8,128)(2,1)S(1)} %collective-permute-done.27.g_p, ...), custom_call_target="tpu_custom_call" | custom-call | flops 805306368 | bytes 4194304 | tf_op jit(solution)/shard_map/square0/pallas_call | solution.py:68
  114.7 8.3 %collective-permute-start.31 = (f32[512,256]{1,0:T(8,128)S(1)}, f32[512,256]{1,0:T(8,128)S(1)}, u32[]{:S(2)}, u32[]{:S(2)}) collective-permute-start(f32[512,256]{1,0:T(8,128)S(1)} %get-tuple-element.95), channel_id=1, source_target_pairs={{0,1},{1,0},{2,3},{3,2},{4,5},{5,4},{6,7},{7,6},{8,9},{9,8},{10,11... | collective-permute-start | bytes 1572872 | tf_op jit(solution)/shard_map/ppermute | solution.py:19
  123.1 1.6 %square1.1 = (f32[512,256]{1,0:T(8,128)S(1)}, f32[512,256]{1,0:T(8,128)S(1)}) custom-call(s32[4]{0:T(128)S(1)} %pad_add_fusion.place, bf16[3,512,512]{2,1,0:T(8,128)(2,1)S(1)} %act_join.1.acts, bf16[2,384,256]{2,1,0:T(8,128)(2,1)S(1)} %grad_join1.1.g, bf16[2,384,256]{2,1,0:T(8,128)(2,1)S(1)} %collective-permute-done.35.g_p, ...), custom_call_target="tpu_custom_call" | custom-call | flops 805306368 | bytes 4194304 | tf_op jit(solution)/shard_map/square1/pallas_call | solution.py:68
  124.7 3.3 %collective-permute-start.39 = (f32[512,256]{1,0:T(8,128)S(1)}, f32[512,256]{1,0:T(8,128)S(1)}, u32[]{:S(2)}, u32[]{:S(2)}) collective-permute-start(f32[512,256]{1,0:T(8,128)S(1)} %get-tuple-element.98), channel_id=1, source_target_pairs={{0,1},{1,0},{2,3},{3,2},{4,5},{5,4},{6,7},{7,6},{8,9},{9,8},{10,11... | collective-permute-start | bytes 1572872 | tf_op jit(solution)/shard_map/ppermute | solution.py:19
  127.9 1.5 %collective-permute-done.39.refs_3_ = f32[512,256]{1,0:T(8,128)S(1)} collective-permute-done((f32[512,256]{1,0:T(8,128)S(1)}, f32[512,256]{1,0:T(8,128)S(1)}, u32[]{:S(2)}, u32[]{:S(2)}) %collective-permute-start.39) | collective-permute-done | bytes 524320 | tf_op jit(solution)/shard_map/ppermute | solution.py:19
  129.5 1.6 %mean.1 = f32[1024,256]{1,0:T(8,128)} custom-call(s32[4]{0:T(128)S(1)} %pad_add_fusion.place, f32[512,256]{1,0:T(8,128)S(1)} %get-tuple-element.94.refs_0_, f32[512,256]{1,0:T(8,128)S(1)} %collective-permute-done.31.refs_1_, f32[512,256]{1,0:T(8,128)S(1)} %get-tuple-element.97.refs_2_, f32[512,256]{1,0:T(8,128)S(1)} %collective-permute-done.39.refs_3_), custom_call_target="tpu_custom_call" | custom-call | bytes 3145728 | tf_op jit(solution)/shard_map/mean/pallas_call | solution.py:68
  (47 shorter events, 1.1 us)
Async XLA Ops:
  0.0 5.0 %collective-permute-start = (bf16[1024,256]{1,0:T(8,128)(2,1)}, bf16[1024,256]{1,0:T(8,128)(2,1)S(1)}, u32[]{:S(2)}, u32[]{:S(2)}) collective-permute-start(bf16[1024,256]{1,0:T(8,128)(2,1)} %ab_own.1), channel_id=1, source_target_pairs={{0,1},{1,0},{2,3},{3,2},{4,5},{5,4},{6,7},{7,6},{8,9},{9,8},{10,11... | collective-permute-start | bytes 1572872 | tf_op jit(solution)/shard_map/ppermute | solution.py:19
  5.0 7.9 %collective-permute-start.1 = (bf16[3072,256]{1,0:T(8,128)(2,1)}, bf16[3072,256]{1,0:T(8,128)(2,1)S(1)}, u32[]{:S(2)}, u32[]{:S(2)}) collective-permute-start(bf16[3072,256]{1,0:T(8,128)(2,1)} %own.3), channel_id=1, source_target_pairs={{0,1},{1,0},{2,3},{3,2},{4,5},{5,4},{6,7},{7,6},{8,9},{9,8},{10,11... | collective-permute-start | bytes 4718600 | tf_op jit(solution)/shard_map/ppermute | solution.py:19
  5.4 7.6 %collective-permute-start.2 = (bf16[256,1024]{1,0:T(8,128)(2,1)}, bf16[256,1024]{1,0:T(8,128)(2,1)S(1)}, u32[]{:S(2)}, u32[]{:S(2)}) collective-permute-start(bf16[256,1024]{1,0:T(8,128)(2,1)} %gb_own.3), channel_id=1, source_target_pairs={{0,1},{1,0},{2,3},{3,2},{4,5},{5,4},{6,7},{7,6},{8,9},{9,8},{10,11... | collective-permute-start | bytes 1572872 | tf_op jit(solution)/shard_map/ppermute | solution.py:19
  5.6 2.8 %copy-start = (bf16[3072,1024]{1,0:T(8,128)(2,1)S(1)}, bf16[3072,1024]{1,0:T(8,128)(2,1)}, u32[]{:S(2)}) copy-start(bf16[3072,1024]{1,0:T(8,128)(2,1)} %acts.1) | copy-start | bytes 18874372
  8.4 1.0 copy-start.3
  9.4 3.5 %copy-start.1 = (bf16[3072,256]{1,0:T(8,128)(2,1)S(1)}, bf16[3072,256]{1,0:T(8,128)(2,1)}, u32[]{:S(2)}) copy-start(bf16[3072,256]{1,0:T(8,128)(2,1)} %own.3) | copy-start | bytes 4718596
  9.4 3.5 %copy-start.2 = (bf16[256,1024]{1,0:T(8,128)(2,1)S(1)}, bf16[256,1024]{1,0:T(8,128)(2,1)}, u32[]{:S(2)}) copy-start(bf16[256,1024]{1,0:T(8,128)(2,1)} %gb_own.3) | copy-start | bytes 1572868
  12.1 7.6 %collective-permute-start.3 = (bf16[400,256]{1,0:T(8,128)(2,1)S(1)}, bf16[400,256]{1,0:T(8,128)(2,1)S(1)}, u32[]{:S(2)}, u32[]{:S(2)}) collective-permute-start(bf16[400,256]{1,0:T(8,128)(2,1)S(1)} %get-tuple-element.62), channel_id=1, source_target_pairs={{0,192},{32,224},{64,128},{96,160},{128,64},{160,96},{192,0},{224,... | collective-permute-start | bytes 614408 | tf_op jit(solution)/shard_map/ppermute | solution.py:24
  12.9 6.8 %collective-permute-start.4 = (bf16[400,256]{1,0:T(8,128)(2,1)S(1)}, bf16[400,256]{1,0:T(8,128)(2,1)S(1)}, u32[]{:S(2)}, u32[]{:S(2)}) collective-permute-start(bf16[400,256]{1,0:T(8,128)(2,1)S(1)} %get-tuple-element.63), channel_id=1, source_target_pairs={{0,64},{32,96},{64,0},{96,32},{128,192},{160,224},{192,128},{224,1... | collective-permute-start | bytes 614408 | tf_op jit(solution)/shard_map/ppermute | solution.py:24
  14.8 12.6 %collective-permute-start.5 = (bf16[400,512]{1,0:T(8,128)(2,1)S(1)}, bf16[400,512]{1,0:T(8,128)(2,1)S(1)}, u32[]{:S(2)}, u32[]{:S(2)}) collective-permute-start(bf16[400,512]{1,0:T(8,128)(2,1)S(1)} %get-tuple-element.56), channel_id=1, source_target_pairs={{0,6},{1,7},{2,4},{3,5},{4,2},{5,3},{6,0},{7,1},{8,14},{9,15},{10,... | collective-permute-start | bytes 1228808 | tf_op jit(solution)/shard_map/ppermute | solution.py:19
  17.6 9.8 %collective-permute-start.6 = (bf16[400,512]{1,0:T(8,128)(2,1)S(1)}, bf16[400,512]{1,0:T(8,128)(2,1)S(1)}, u32[]{:S(2)}, u32[]{:S(2)}) collective-permute-start(bf16[400,512]{1,0:T(8,128)(2,1)S(1)} %get-tuple-element.67), channel_id=1, source_target_pairs={{0,2},{1,3},{2,0},{3,1},{4,6},{5,7},{6,4},{7,5},{8,10},{9,11},{10,... | collective-permute-start | bytes 1228808 | tf_op jit(solution)/shard_map/ppermute | solution.py:19
  21.5 12.4 %collective-permute-start.8 = (bf16[400,512]{1,0:T(8,128)(2,1)S(1)}, bf16[400,512]{1,0:T(8,128)(2,1)S(1)}, u32[]{:S(2)}, u32[]{:S(2)}) collective-permute-start(bf16[400,512]{1,0:T(8,128)(2,1)S(1)} %get-tuple-element.72), channel_id=1, source_target_pairs={{0,192},{32,224},{64,128},{96,160},{128,64},{160,96},{192,0},{224,... | collective-permute-start | bytes 1228808 | tf_op jit(solution)/shard_map/ppermute | solution.py:24
  22.7 12.1 %collective-permute-start.7 = (bf16[400,512]{1,0:T(8,128)(2,1)S(1)}, bf16[400,512]{1,0:T(8,128)(2,1)S(1)}, u32[]{:S(2)}, u32[]{:S(2)}) collective-permute-start(bf16[400,512]{1,0:T(8,128)(2,1)S(1)} %get-tuple-element.64), channel_id=1, source_target_pairs={{0,64},{32,96},{64,0},{96,32},{128,192},{160,224},{192,128},{224,1... | collective-permute-start | bytes 1228808 | tf_op jit(solution)/shard_map/ppermute | solution.py:24
  29.3 14.1 %collective-permute-start.10 = (bf16[400,512]{1,0:T(8,128)(2,1)S(1)}, bf16[400,512]{1,0:T(8,128)(2,1)S(1)}, u32[]{:S(2)}, u32[]{:S(2)}) collective-permute-start(bf16[400,512]{1,0:T(8,128)(2,1)S(1)} %get-tuple-element.76), channel_id=1, source_target_pairs={{0,6},{1,7},{2,4},{3,5},{4,2},{5,3},{6,0},{7,1},{8,14},{9,15},{10,... | collective-permute-start | bytes 1228808 | tf_op jit(solution)/shard_map/ppermute | solution.py:19
  30.9 12.5 %collective-permute-start.9 = (bf16[400,512]{1,0:T(8,128)(2,1)S(1)}, bf16[400,512]{1,0:T(8,128)(2,1)S(1)}, u32[]{:S(2)}, u32[]{:S(2)}) collective-permute-start(bf16[400,512]{1,0:T(8,128)(2,1)S(1)} %get-tuple-element.68), channel_id=1, source_target_pairs={{0,2},{1,3},{2,0},{3,1},{4,6},{5,7},{6,4},{7,5},{8,10},{9,11},{10,... | collective-permute-start | bytes 1228808 | tf_op jit(solution)/shard_map/ppermute | solution.py:19
  32.7 15.6 %collective-permute-start.12 = (bf16[400,512]{1,0:T(8,128)(2,1)S(1)}, bf16[400,512]{1,0:T(8,128)(2,1)S(1)}, u32[]{:S(2)}, u32[]{:S(2)}) collective-permute-start(bf16[400,512]{1,0:T(8,128)(2,1)S(1)} %get-tuple-element.79), channel_id=1, source_target_pairs={{0,6},{1,7},{2,4},{3,5},{4,2},{5,3},{6,0},{7,1},{8,14},{9,15},{10,... | collective-permute-start | bytes 1228808 | tf_op jit(solution)/shard_map/ppermute | solution.py:19
  33.9 18.7 %collective-permute-start.11 = (bf16[400,512]{1,0:T(8,128)(2,1)S(1)}, bf16[400,512]{1,0:T(8,128)(2,1)S(1)}, u32[]{:S(2)}, u32[]{:S(2)}) collective-permute-start(bf16[400,512]{1,0:T(8,128)(2,1)S(1)} %get-tuple-element.70), channel_id=1, source_target_pairs={{0,2},{1,3},{2,0},{3,1},{4,6},{5,7},{6,4},{7,5},{8,10},{9,11},{10,... | collective-permute-start | bytes 1228808 | tf_op jit(solution)/shard_map/ppermute | solution.py:19
  36.3 26.6 %collective-permute-start.16 = (bf16[400,256]{1,0:T(8,128)(2,1)S(1)}, bf16[400,256]{1,0:T(8,128)(2,1)S(1)}, u32[]{:S(2)}, u32[]{:S(2)}) collective-permute-start(bf16[400,256]{1,0:T(8,128)(2,1)S(1)} %get-tuple-element.86), channel_id=1, source_target_pairs={{0,32},{32,0},{64,96},{96,64},{128,160},{160,128},{192,224},{224,1... | collective-permute-start | bytes 614408 | tf_op jit(solution)/shard_map/ppermute | solution.py:24
  45.0 13.4 %collective-permute-start.13 = (bf16[112,512]{1,0:T(8,128)(2,1)S(1)}, bf16[112,512]{1,0:T(8,128)(2,1)S(1)}, u32[]{:S(2)}, u32[]{:S(2)}) collective-permute-start(bf16[112,512]{1,0:T(8,128)(2,1)S(1)} %get-tuple-element.82), channel_id=1, source_target_pairs={{0,8},{1,9},{2,10},{3,11},{4,12},{5,13},{6,14},{7,15},{8,0},{9,1},... | collective-permute-start | bytes 344072 | tf_op jit(solution)/shard_map/ppermute | solution.py:19
  45.8 12.7 %collective-permute-start.14 = (bf16[112,512]{1,0:T(8,128)(2,1)S(1)}, bf16[112,512]{1,0:T(8,128)(2,1)S(1)}, u32[]{:S(2)}, u32[]{:S(2)}) collective-permute-start(bf16[112,512]{1,0:T(8,128)(2,1)S(1)} %get-tuple-element.83), channel_id=1, source_target_pairs={{0,16},{1,17},{2,18},{3,19},{4,20},{5,21},{6,22},{7,23},{8,24},{9,... | collective-permute-start | bytes 344072 | tf_op jit(solution)/shard_map/ppermute | solution.py:19
  48.2 12.2 %collective-permute-start.15 = (bf16[112,512]{1,0:T(8,128)(2,1)S(1)}, bf16[112,512]{1,0:T(8,128)(2,1)S(1)}, u32[]{:S(2)}, u32[]{:S(2)}) collective-permute-start(bf16[112,512]{1,0:T(8,128)(2,1)S(1)} %get-tuple-element.84), channel_id=1, source_target_pairs={{0,24},{1,25},{2,26},{3,27},{4,28},{5,29},{6,30},{7,31},{8,16},{9,... | collective-permute-start | bytes 344072 | tf_op jit(solution)/shard_map/ppermute | solution.py:19
  52.6 16.4 %collective-permute-start.17 = (bf16[400,256]{1,0:T(8,128)(2,1)S(1)}, bf16[400,256]{1,0:T(8,128)(2,1)S(1)}, u32[]{:S(2)}, u32[]{:S(2)}) collective-permute-start(bf16[400,256]{1,0:T(8,128)(2,1)S(1)} %get-tuple-element.87), channel_id=1, source_target_pairs={{0,32},{32,0},{64,96},{96,64},{128,160},{160,128},{192,224},{224,1... | collective-permute-start | bytes 614408 | tf_op jit(solution)/shard_map/ppermute | solution.py:24
  58.4 12.4 %collective-permute-start.18 = (bf16[112,512]{1,0:T(8,128)(2,1)S(1)}, bf16[112,512]{1,0:T(8,128)(2,1)S(1)}, u32[]{:S(2)}, u32[]{:S(2)}) collective-permute-start(bf16[112,512]{1,0:T(8,128)(2,1)S(1)} %get-tuple-element.89), channel_id=1, source_target_pairs={{0,8},{1,9},{2,10},{3,11},{4,12},{5,13},{6,14},{7,15},{8,0},{9,1},... | collective-permute-start | bytes 344072 | tf_op jit(solution)/shard_map/ppermute | solution.py:19
  58.5 21.2 %collective-permute-start.19 = (bf16[112,512]{1,0:T(8,128)(2,1)S(1)}, bf16[112,512]{1,0:T(8,128)(2,1)S(1)}, u32[]{:S(2)}, u32[]{:S(2)}) collective-permute-start(bf16[112,512]{1,0:T(8,128)(2,1)S(1)} %get-tuple-element.90), channel_id=1, source_target_pairs={{0,16},{1,17},{2,18},{3,19},{4,20},{5,21},{6,22},{7,23},{8,24},{9,... | collective-permute-start | bytes 344072 | tf_op jit(solution)/shard_map/ppermute | solution.py:19
  60.4 20.7 %collective-permute-start.20 = (bf16[112,512]{1,0:T(8,128)(2,1)S(1)}, bf16[112,512]{1,0:T(8,128)(2,1)S(1)}, u32[]{:S(2)}, u32[]{:S(2)}) collective-permute-start(bf16[112,512]{1,0:T(8,128)(2,1)S(1)} %get-tuple-element.91), channel_id=1, source_target_pairs={{0,24},{1,25},{2,26},{3,27},{4,28},{5,29},{6,30},{7,31},{8,16},{9,... | collective-permute-start | bytes 344072 | tf_op jit(solution)/shard_map/ppermute | solution.py:19
  62.9 21.1 %collective-permute-start.23 = (bf16[96,512]{1,0:T(8,128)(2,1)S(1)}, bf16[96,512]{1,0:T(8,128)(2,1)S(1)}, u32[]{:S(2)}, u32[]{:S(2)}) collective-permute-start(bf16[96,512]{1,0:T(8,128)(2,1)S(1)} %grad_round0.1.g0), channel_id=1, source_target_pairs={{0,24},{1,25},{2,26},{3,27},{4,28},{5,29},{6,30},{7,31},{8,16},{9,... | collective-permute-start | bytes 294920 | tf_op jit(solution)/shard_map/ppermute | solution.py:19
  69.9 20.5 %collective-permute-start.26 = (bf16[384,512]{1,0:T(8,128)(2,1)S(1)}, bf16[384,512]{1,0:T(8,128)(2,1)S(1)}, u32[]{:S(2)}, u32[]{:S(2)}) collective-permute-start(bf16[384,512]{1,0:T(8,128)(2,1)S(1)} %act_round.1.a0), channel_id=1, source_target_pairs={{0,192},{32,224},{64,128},{96,160},{128,64},{160,96},{192,0},{224,... | collective-permute-start | bytes 1179656 | tf_op jit(solution)/shard_map/ppermute | solution.py:24
  70.8 22.4 %collective-permute-start.25 = (bf16[384,512]{1,0:T(8,128)(2,1)S(1)}, bf16[384,512]{1,0:T(8,128)(2,1)S(1)}, u32[]{:S(2)}, u32[]{:S(2)}) collective-permute-start(bf16[384,512]{1,0:T(8,128)(2,1)S(1)} %act_round.1.a0), channel_id=1, source_target_pairs={{0,128},{32,160},{64,192},{96,224},{128,0},{160,32},{192,64},{224,... | collective-permute-start | bytes 1179656 | tf_op jit(solution)/shard_map/ppermute | solution.py:24
  79.8 13.4 %collective-permute-start.24 = (bf16[384,512]{1,0:T(8,128)(2,1)S(1)}, bf16[384,512]{1,0:T(8,128)(2,1)S(1)}, u32[]{:S(2)}, u32[]{:S(2)}) collective-permute-start(bf16[384,512]{1,0:T(8,128)(2,1)S(1)} %act_round.1.a0), channel_id=1, source_target_pairs={{0,64},{32,96},{64,0},{96,32},{128,192},{160,224},{192,128},{224,1... | collective-permute-start | bytes 1179656 | tf_op jit(solution)/shard_map/ppermute | solution.py:24
  81.1 5.4 %collective-permute-start.22 = (bf16[96,512]{1,0:T(8,128)(2,1)S(1)}, bf16[96,512]{1,0:T(8,128)(2,1)S(1)}, u32[]{:S(2)}, u32[]{:S(2)}) collective-permute-start(bf16[96,512]{1,0:T(8,128)(2,1)S(1)} %grad_round0.1.g0), channel_id=1, source_target_pairs={{0,16},{1,17},{2,18},{3,19},{4,20},{5,21},{6,22},{7,23},{8,24},{9,... | collective-permute-start | bytes 294920 | tf_op jit(solution)/shard_map/ppermute | solution.py:19
  84.0 3.8 %collective-permute-start.21 = (bf16[96,512]{1,0:T(8,128)(2,1)S(1)}, bf16[96,512]{1,0:T(8,128)(2,1)S(1)}, u32[]{:S(2)}, u32[]{:S(2)}) collective-permute-start(bf16[96,512]{1,0:T(8,128)(2,1)S(1)} %grad_round0.1.g0), channel_id=1, source_target_pairs={{0,8},{1,9},{2,10},{3,11},{4,12},{5,13},{6,14},{7,15},{8,0},{9,1},... | collective-permute-start | bytes 294920 | tf_op jit(solution)/shard_map/ppermute | solution.py:19
  88.4 11.8 %collective-permute-start.28 = (bf16[2,384,256]{2,1,0:T(8,128)(2,1)S(1)}, bf16[2,384,256]{2,1,0:T(8,128)(2,1)S(1)}, u32[]{:S(2)}, u32[]{:S(2)}) collective-permute-start(bf16[2,384,256]{2,1,0:T(8,128)(2,1)S(1)} %grad_join0.1.g), channel_id=1, source_target_pairs={{0,6},{1,7},{2,4},{3,5},{4,2},{5,3},{6,0},{7,1},{8,14},{9,15},{10,... | collective-permute-start | bytes 1179656 | tf_op jit(solution)/shard_map/ppermute | solution.py:19
  90.1 11.5 %collective-permute-start.27 = (bf16[2,384,256]{2,1,0:T(8,128)(2,1)S(1)}, bf16[2,384,256]{2,1,0:T(8,128)(2,1)S(1)}, u32[]{:S(2)}, u32[]{:S(2)}) collective-permute-start(bf16[2,384,256]{2,1,0:T(8,128)(2,1)S(1)} %grad_join0.1.g), channel_id=1, source_target_pairs={{0,2},{1,3},{2,0},{3,1},{4,6},{5,7},{6,4},{7,5},{8,10},{9,11},{10,... | collective-permute-start | bytes 1179656 | tf_op jit(solution)/shard_map/ppermute | solution.py:19
  90.5 5.3 %collective-permute-start.34 = (bf16[96,512]{1,0:T(8,128)(2,1)S(1)}, bf16[96,512]{1,0:T(8,128)(2,1)S(1)}, u32[]{:S(2)}, u32[]{:S(2)}) collective-permute-start(bf16[96,512]{1,0:T(8,128)(2,1)S(1)} %grad_round1.1.g0), channel_id=1, source_target_pairs={{0,24},{1,25},{2,26},{3,27},{4,28},{5,29},{6,30},{7,31},{8,16},{9,... | collective-permute-start | bytes 294920 | tf_op jit(solution)/shard_map/ppermute | solution.py:19
  93.2 4.6 %collective-permute-start.33 = (bf16[96,512]{1,0:T(8,128)(2,1)S(1)}, bf16[96,512]{1,0:T(8,128)(2,1)S(1)}, u32[]{:S(2)}, u32[]{:S(2)}) collective-permute-start(bf16[96,512]{1,0:T(8,128)(2,1)S(1)} %grad_round1.1.g0), channel_id=1, source_target_pairs={{0,16},{1,17},{2,18},{3,19},{4,20},{5,21},{6,22},{7,23},{8,24},{9,... | collective-permute-start | bytes 294920 | tf_op jit(solution)/shard_map/ppermute | solution.py:19
  93.2 4.6 %collective-permute-start.32 = (bf16[96,512]{1,0:T(8,128)(2,1)S(1)}, bf16[96,512]{1,0:T(8,128)(2,1)S(1)}, u32[]{:S(2)}, u32[]{:S(2)}) collective-permute-start(bf16[96,512]{1,0:T(8,128)(2,1)S(1)} %grad_round1.1.g0), channel_id=1, source_target_pairs={{0,8},{1,9},{2,10},{3,11},{4,12},{5,13},{6,14},{7,15},{8,0},{9,1},... | collective-permute-start | bytes 294920 | tf_op jit(solution)/shard_map/ppermute | solution.py:19
  98.4 10.1 %collective-permute-start.36 = (bf16[2,384,256]{2,1,0:T(8,128)(2,1)S(1)}, bf16[2,384,256]{2,1,0:T(8,128)(2,1)S(1)}, u32[]{:S(2)}, u32[]{:S(2)}) collective-permute-start(bf16[2,384,256]{2,1,0:T(8,128)(2,1)S(1)} %grad_join1.1.g), channel_id=1, source_target_pairs={{0,6},{1,7},{2,4},{3,5},{4,2},{5,3},{6,0},{7,1},{8,14},{9,15},{10,... | collective-permute-start | bytes 1179656 | tf_op jit(solution)/shard_map/ppermute | solution.py:19
  100.0 10.1 %collective-permute-start.35 = (bf16[2,384,256]{2,1,0:T(8,128)(2,1)S(1)}, bf16[2,384,256]{2,1,0:T(8,128)(2,1)S(1)}, u32[]{:S(2)}, u32[]{:S(2)}) collective-permute-start(bf16[2,384,256]{2,1,0:T(8,128)(2,1)S(1)} %grad_join1.1.g), channel_id=1, source_target_pairs={{0,2},{1,3},{2,0},{3,1},{4,6},{5,7},{6,4},{7,5},{8,10},{9,11},{10,... | collective-permute-start | bytes 1179656 | tf_op jit(solution)/shard_map/ppermute | solution.py:19
  100.2 13.0 %collective-permute-start.30 = (bf16[384,256]{1,0:T(8,128)(2,1)S(1)}, bf16[384,256]{1,0:T(8,128)(2,1)S(1)}, u32[]{:S(2)}, u32[]{:S(2)}) collective-permute-start(bf16[384,256]{1,0:T(8,128)(2,1)S(1)} %slice_bitcast_fusion.2), channel_id=1, source_target_pairs={{0,2},{1,3},{2,0},{3,1},{4,6},{5,7},{6,4},{7,5},{8,10},{9,11},{10,... | collective-permute-start | bytes 589832 | tf_op jit(solution)/shard_map/ppermute | solution.py:19
  101.6 11.5 %collective-permute-start.29 = (bf16[384,256]{1,0:T(8,128)(2,1)S(1)}, bf16[384,256]{1,0:T(8,128)(2,1)S(1)}, u32[]{:S(2)}, u32[]{:S(2)}) collective-permute-start(bf16[384,256]{1,0:T(8,128)(2,1)S(1)} %slice_bitcast_fusion.3), channel_id=1, source_target_pairs={{0,6},{1,7},{2,4},{3,5},{4,2},{5,3},{6,0},{7,1},{8,14},{9,15},{10,... | collective-permute-start | bytes 589832 | tf_op jit(solution)/shard_map/ppermute | solution.py:19
  108.5 14.5 %collective-permute-start.38 = (bf16[384,256]{1,0:T(8,128)(2,1)S(1)}, bf16[384,256]{1,0:T(8,128)(2,1)S(1)}, u32[]{:S(2)}, u32[]{:S(2)}) collective-permute-start(bf16[384,256]{1,0:T(8,128)(2,1)S(1)} %slice_bitcast_fusion), channel_id=1, source_target_pairs={{0,2},{1,3},{2,0},{3,1},{4,6},{5,7},{6,4},{7,5},{8,10},{9,11},{10,... | collective-permute-start | bytes 589832 | tf_op jit(solution)/shard_map/ppermute | solution.py:19
  110.2 12.9 %collective-permute-start.37 = (bf16[384,256]{1,0:T(8,128)(2,1)S(1)}, bf16[384,256]{1,0:T(8,128)(2,1)S(1)}, u32[]{:S(2)}, u32[]{:S(2)}) collective-permute-start(bf16[384,256]{1,0:T(8,128)(2,1)S(1)} %slice_bitcast_fusion.1), channel_id=1, source_target_pairs={{0,6},{1,7},{2,4},{3,5},{4,2},{5,3},{6,0},{7,1},{8,14},{9,15},{10,... | collective-permute-start | bytes 589832 | tf_op jit(solution)/shard_map/ppermute | solution.py:19
  114.7 13.2 %collective-permute-start.31 = (f32[512,256]{1,0:T(8,128)S(1)}, f32[512,256]{1,0:T(8,128)S(1)}, u32[]{:S(2)}, u32[]{:S(2)}) collective-permute-start(f32[512,256]{1,0:T(8,128)S(1)} %get-tuple-element.95), channel_id=1, source_target_pairs={{0,1},{1,0},{2,3},{3,2},{4,5},{5,4},{6,7},{7,6},{8,9},{9,8},{10,11... | collective-permute-start | bytes 1572872 | tf_op jit(solution)/shard_map/ppermute | solution.py:19
  124.7 4.8 %collective-permute-start.39 = (f32[512,256]{1,0:T(8,128)S(1)}, f32[512,256]{1,0:T(8,128)S(1)}, u32[]{:S(2)}, u32[]{:S(2)}) collective-permute-start(f32[512,256]{1,0:T(8,128)S(1)} %get-tuple-element.98), channel_id=1, source_target_pairs={{0,1},{1,0},{2,3},{3,2},{4,5},{5,4},{6,7},{7,6},{8,9},{9,8},{10,11... | collective-permute-start | bytes 1572872 | tf_op jit(solution)/shard_map/ppermute | solution.py:19
